TPU v7x, 256 devices: a whole 4x4x8 slice. The times are simulated.
256 devices in a mesh: fsdp: 32 (over x, z_hi, core), tp: 8 (over z_lo, y).
Axes of the slice: x: 4, y: 4, z: 8 (z_hi: 4, z_lo: 2; z = z_hi * 2 + z_lo), core: 2. Of those that a mesh axis runs over, the one named last changes fastest.
Arguments:
- master: float32 [8192, 2048], P('fsdp', 'tp'), may hold values from -0.0625 to 0.0625
- grad: bfloat16 [8192, 2048], P('fsdp', 'tp'), may hold values from -6 to 6
- moment: float32 [8192, 2048], P('fsdp', 'tp'), may hold values from -4 to 4
- variance: float32 [8192, 2048], P('fsdp', 'tp'), may hold values from 0.01 to 1
- q_left: bfloat16 [8192, 8192], P(None, 'fsdp'), may hold values from -0.0625 to 0.0625
- q_right: bfloat16 [2048, 2048], P(None, 'tp'), may hold values from -0.125 to 0.125
- embed: bfloat16 [76032, 8192], P('tp', 'fsdp')
- gain: float32 [8192], replicated, may hold values from 0.5 to 1.5
- token_ids: int32 [128, 4], replicated, may hold values from 0 to 76031
- queries: bfloat16 [128, 4, 8192], P('fsdp', None, 'tp')
- k_cache: bfloat16 [128, 8, 512, 128], P('fsdp', 'tp')
- v_cache: bfloat16 [128, 8, 512, 128], P('fsdp', 'tp'), may hold values from -6 to 6
- cache_len: int32 [128], P('fsdp'), may hold values from 1 to 512, as said below
Outputs:
- update: float32 [8192, 2048], P('fsdp', 'tp')
- moment_new: float32 [8192, 2048], P('fsdp', 'tp')
- variance_new: float32 [8192, 2048], P('fsdp', 'tp')
- attended: float32 [128, 4, 8192], P('fsdp', None, 'tp')
Inputs may be any that keep to these rules, and one draw needn't show every extreme that they name: `cache_len`: at least one sequence has exactly 512 cached positions.
All inputs are finite; a program needn't handle non-finite values.
Results may differ from a plain program's by a relative error of at most 0.022.
Values may be sent and summed in bfloat16 or wider, within the bound.
No kernel may reach another device: no remote copies, remote signals or barrier semaphores. Data moves between devices by JAX's collectives and lax.ppermute only.
A program may use at most 64 MiB of HBM per device.

v0:
```python
import jax
import jax.numpy as jnp
from jax import lax
from jax.sharding import PartitionSpec as P

beta_one = 0.9
beta_two = 0.95
adam_eps = 1e-08
learn_rate = 0.003
adam_step = 20
norm_eps = 1e-06
rope_base = 1000000.0


def rotary(vectors, positions):
    head_dim = vectors.shape[-1]
    half_dim = head_dim // 2
    inverse = rope_base ** (-(jnp.arange(half_dim, dtype=jnp.float32) * 2.0 / head_dim))
    angles = positions[..., None].astype(jnp.float32) * inverse
    cosine = jnp.cos(angles)
    sine_part = jnp.sin(angles)
    first_half = vectors[..., :half_dim]
    second_half = vectors[..., half_dim:]
    return jnp.concatenate(
        [
            first_half * cosine - second_half * sine_part,
            second_half * cosine + first_half * sine_part,
        ],
        -1,
    )


def attend(queries, k_cache, v_cache, k_new, v_new, cache_len):
    seqs = queries.shape[0]
    steps = queries.shape[1]
    heads_kv = k_cache.shape[1]
    head_dim = k_cache.shape[3]
    scaling = float(head_dim) ** (-0.5)
    query_f = queries.reshape(seqs, steps, heads_kv, -1, head_dim)
    score_old = (
        jnp.einsum("stkgd,skcd->sktgc", query_f, k_cache, preferred_element_type=jnp.float32)
        * scaling
    )
    score_new = (
        jnp.einsum("stkgd,sjkd->sktgj", query_f, k_new, preferred_element_type=jnp.float32)
        * scaling
    )
    old_mask = (jnp.arange(k_cache.shape[2], dtype=jnp.int32)[None, :] < cache_len[:, None])[
        :, None, None, None, :
    ]
    step_ids = jnp.arange(steps, dtype=jnp.int32)
    new_mask = (step_ids[None, :] <= step_ids[:, None])[None, None, :, None, :]
    score_old = jnp.where(old_mask, score_old, -1e30)
    score_new = jnp.where(new_mask, score_new, -1e30)
    row_max = jnp.maximum(jnp.max(score_old, -1), jnp.max(score_new, -1))[..., None]
    exp_old = jnp.where(old_mask, jnp.exp(score_old - row_max), 0.0)
    exp_new = jnp.where(new_mask, jnp.exp(score_new - row_max), 0.0)
    totals = jnp.sum(exp_old, -1, keepdims=True) + jnp.sum(exp_new, -1, keepdims=True)
    prob_old = (exp_old / totals).astype(jnp.bfloat16)
    prob_new = (exp_new / totals).astype(jnp.bfloat16)
    output = jnp.einsum("sktgc,skcd->stkgd", prob_old, v_cache, preferred_element_type=jnp.float32)
    output = output + jnp.einsum(
        "sktgj,sjkd->stkgd", prob_new, v_new, preferred_element_type=jnp.float32
    )
    return output.reshape(seqs, steps, -1)


def contract_first(left_op, right_op):
    return lax.dot_general(
        left_op, right_op, (((0,), (0,)), ((), ())), preferred_element_type=jnp.float32
    )


def contract_last(left_op, right_op):
    return lax.dot_general(
        left_op, right_op, (((1,), (1,)), ((), ())), preferred_element_type=jnp.float32
    )


def shards(
    master,
    grad,
    moment,
    variance,
    q_left,
    q_right,
    embed,
    gain,
    token_ids,
    queries,
    k_cache,
    v_cache,
    cache_len,
):
    moment_new = beta_one * moment + (1.0 - beta_one) * grad.astype(jnp.float32)
    moment_low = moment_new.astype(jnp.bfloat16)
    pieces = (
        lax.all_gather(grad, "fsdp", axis=0, tiled=True),
        lax.all_gather(moment_low, "fsdp", axis=0, tiled=True),
    )
    left_block = q_left
    left_g = contract_first(left_block, pieces[0])
    left_m = contract_first(left_block, pieces[1])
    pieces = (
        lax.all_gather(left_g.astype(jnp.bfloat16), "tp", axis=1, tiled=True),
        lax.all_gather(left_m.astype(jnp.bfloat16), "tp", axis=1, tiled=True),
    )
    right_block = q_right
    rot_g = jnp.dot(pieces[0], right_block, preferred_element_type=jnp.float32)
    rot_m = jnp.dot(pieces[1], right_block, preferred_element_type=jnp.float32)
    variance_new = beta_two * variance + (1.0 - beta_two) * rot_g * rot_g
    corr_one = 1.0 - beta_one**adam_step
    corr_two = 1.0 - beta_two**adam_step
    direction = (rot_m / corr_one / (jnp.sqrt(variance_new / corr_two) + adam_eps)).astype(
        jnp.bfloat16
    )
    right_block = q_right
    back_rows = lax.psum_scatter(
        contract_last(right_block, direction).astype(jnp.bfloat16),
        "tp",
        scatter_dimension=0,
        tiled=True,
    )
    left_block = q_left
    update = lax.psum_scatter(
        contract_last(left_block, back_rows).astype(jnp.bfloat16),
        "fsdp",
        scatter_dimension=0,
        tiled=True,
    ).astype(jnp.float32)
    weight = (master - learn_rate * update).astype(jnp.bfloat16)
    flat_ids = token_ids.reshape(-1)
    vocab_rows = embed.shape[0]
    local_ids = flat_ids - lax.axis_index("tp") * vocab_rows
    inside = (local_ids >= 0) & (local_ids < vocab_rows)
    picked = jnp.take(embed, jnp.clip(local_ids, 0, vocab_rows - 1), axis=0)
    picked = jnp.where(inside[:, None], picked, jnp.zeros_like(picked))
    looked_up = lax.psum(picked.astype(jnp.float32).astype(jnp.bfloat16), "tp")
    seq_here = queries.shape[0]
    steps = queries.shape[1]
    token_feats = lax.all_to_all(looked_up, "fsdp", split_axis=0, concat_axis=1, tiled=True)
    features = token_feats.astype(jnp.float32)
    mean_square = jnp.mean(features * features, -1, keepdims=True)
    normed = (features * lax.rsqrt(mean_square + norm_eps) * gain).astype(jnp.bfloat16)
    key_value = jnp.dot(
        normed,
        lax.all_gather(weight, "fsdp", axis=0, tiled=True),
        preferred_element_type=jnp.float32,
    )
    heads_here = k_cache.shape[1]
    head_dim = k_cache.shape[3]
    key_value = key_value.reshape(seq_here, steps, heads_here, 2, head_dim)
    positions = cache_len[:, None] + jnp.arange(steps, dtype=jnp.int32)[None, :]
    k_new = rotary(key_value[:, :, :, 0], positions[:, :, None]).astype(jnp.bfloat16)
    v_new = key_value[:, :, :, 1].astype(jnp.bfloat16)
    attended = attend(queries, k_cache, v_cache, k_new, v_new, cache_len)
    return (update, moment_new, variance_new, attended)


def solution(mesh):
    in_specs = (
        P("fsdp", "tp"),
        P("fsdp", "tp"),
        P("fsdp", "tp"),
        P("fsdp", "tp"),
        P(None, "fsdp"),
        P(None, "tp"),
        P("tp", "fsdp"),
        P(),
        P(),
        P("fsdp", None, "tp"),
        P("fsdp", "tp", None, None),
        P("fsdp", "tp", None, None),
        P("fsdp"),
    )
    out_specs = (P("fsdp", "tp"), P("fsdp", "tp"), P("fsdp", "tp"), P("fsdp", None, "tp"))
    return jax.shard_map(shards, mesh=mesh, in_specs=in_specs, out_specs=out_specs, check_vma=False)
```

profile of v0, /device:TPU:32, one launch (start us, length us, event | category | flops | bytes accessed | tf_op | source)
XLA Modules:
  0.0 523.7 jit_solution(13208374250276750596)
XLA Ops:
  7.2 0.7 all-gather.10.cloned.1.call-update
  8.0 1.8 fusion.53
  9.8 62.6 %all-gather.10.cloned.1.call-done = bf16[8192,256]{1,0:T(8,128)(2,1)} async-done(((bf16[256,256]{1,0:T(8,128)(2,1)}), bf16[8192,256]{1,0:T(8,128)(2,1)}) %all-gather.10.cloned.1.call-update) | async-done | bytes 4194320 | tf_op jit(solution)/shard_map/all_gather | solution.py:98
  72.5 5.4 %convolution_convert_fusion.2 = bf16[256,256]{1,0:T(8,128)(2,1)} fusion(bf16[8192,256]{1,0:T(8,128)(2,1)} %param.17, bf16[8192,256]{1,0:T(8,128)(2,1)} %all-gather.10.cloned.1.call-done), kind=kOutput, calls=%fused_computation.10 | convolution fusion | flops 1073807360 | bytes 8519680 | tf_op jit(solution)/shard_map/dot_general | solution.py:69
  78.0 55.6 %all-gather.6.cloned.1.call-done = bf16[8192,256]{1,0:T(8,128)(2,1)} async-done(((bf16[256,256]{1,0:T(8,128)(2,1)}), bf16[8192,256]{1,0:T(8,128)(2,1)}) %all-gather.6.cloned.1.call-update) | async-done | bytes 4194320 | tf_op jit(solution)/shard_map/all_gather | solution.py:99
  133.6 5.4 %fusion.5 = bf16[256,256]{0,1:T(8,128)(2,1)} fusion(bf16[8192,256]{1,0:T(8,128)(2,1)} %all-gather.6.cloned.1.call-done, bf16[8192,256]{1,0:T(8,128)(2,1)} %param.17), kind=kOutput, calls=%fused_computation.12 | convolution fusion | flops 1073807360 | bytes 8519680 | tf_op jit(solution)/shard_map/dot_general | solution.py:69
  139.1 34.8 %all-gather.12.cloned.1.call-done = bf16[256,2048]{1,0:T(8,128)(2,1)} async-done(((bf16[256,256]{1,0:T(8,128)(2,1)}), bf16[256,2048]{1,0:T(8,128)(2,1)}) %all-gather.12.cloned.1.call-update) | async-done | bytes 1048592 | tf_op jit(solution)/shard_map/all_gather | solution.py:105
  173.8 1.7 fusion.14
  175.5 42.4 %all-gather.8.cloned.1.call-done = bf16[256,2048]{0,1:T(8,128)(2,1)} async-done(((bf16[256,256]{0,1:T(8,128)(2,1)}), bf16[256,2048]{0,1:T(8,128)(2,1)}) %all-gather.8.cloned.1.call-update) | async-done | bytes 1048592 | tf_op jit(solution)/shard_map/all_gather | solution.py:106
  217.9 3.5 fusion.1
  221.5 40.7 %reduce-scatter.3.cloned.1.call-done = bf16[256,256]{0,1:T(8,128)(2,1)} async-done(((bf16[2048,256]{0,1:T(8,128)(2,1)}), bf16[256,256]{0,1:T(8,128)(2,1)}) %reduce-scatter.3.cloned.1.call-update) | async-done | bytes 131088 | tf_op jit(solution)/shard_map/reduce_scatter | solution.py:118
  262.2 5.5 %fusion = bf16[8192,256]{0,1:T(8,128)(2,1)} fusion(bf16[256,256]{0,1:T(8,128)(2,1)} %reduce-scatter.3.cloned.1.call-done, bf16[8192,256]{1,0:T(8,128)(2,1)} %param.17), kind=kOutput, calls=%fused_computation.2 | convolution fusion | flops 1075838976 | bytes 8519680 | tf_op jit(solution)/shard_map/dot_general | solution.py:75
  267.9 0.6 copy-done.7
  269.1 4.6 gather_fusion
  273.7 0.9 select_select_fusion
  274.8 91.2 %reduce-scatter.5.cloned.1.call-done = bf16[256,256]{0,1:T(8,128)(2,1)} async-done(((bf16[8192,256]{0,1:T(8,128)(2,1)}), bf16[256,256]{0,1:T(8,128)(2,1)}) %reduce-scatter.5.cloned.1.call-update) | async-done | bytes 131088 | tf_op jit(solution)/shard_map/reduce_scatter | solution.py:125
  366.0 1.6 subtract_convert_fusion
  367.7 78.3 %all-reduce.2.cloned.1.call-done = bf16[32,16,256]{2,1,0:T(8,128)(2,1)} async-done(((bf16[32,16,256]{2,1,0:T(8,128)(2,1)}), bf16[32,16,256]{2,1,0:T(8,128)(2,1)}) %all-reduce.2.cloned.1.call-update) | async-done | bytes 262160 | tf_op jit(solution)/shard_map/psum | solution.py:138
  446.1 9.8 %all-to-all-start = ((bf16[32,16,256]{2,1,0:T(8,128)(2,1)}), bf16[32,16,256]{2,1,0:T(8,128)(2,1)S(1)}, u32[]{:S(2)}, u32[]{:S(2)}) async-start(bf16[32,16,256]{2,1,0:T(8,128)(2,1)} %all-reduce.2.cloned.1.call-done), calls=%async_computation.2 | async-start | bytes 524288 | tf_op jit(solution)/shard_map/all_to_all | solution.py:141
  456.4 13.0 %all-to-all-done = bf16[32,16,256]{2,1,0:T(8,128)(2,1)S(1)} async-done(((bf16[32,16,256]{2,1,0:T(8,128)(2,1)}), bf16[32,16,256]{2,1,0:T(8,128)(2,1)S(1)}, u32[]{:S(2)}, u32[]{:S(2)}) %all-to-all-start) | async-done | bytes 262176 | tf_op jit(solution)/shard_map/all_to_all | solution.py:141
  470.0 1.7 copy.25
  471.7 39.6 %all-gather.14.cloned.1.call-done = bf16[8192,256]{0,1:T(8,128)(2,1)} async-done(((bf16[256,256]{0,1:T(8,128)(2,1)}), bf16[8192,256]{0,1:T(8,128)(2,1)}) %all-gather.14.cloned.1.call-update) | async-done | bytes 4194320 | tf_op jit(solution)/shard_map/all_gather | solution.py:147
  511.3 3.5 convolution_bitcast_fusion.1
  516.2 0.7 reshape.276
  (66 shorter events, 3.7 us)
Async XLA Ops:
  7.2 166.7 %copy-start = (bf16[2048,256]{1,0:T(8,128)(2,1)S(1)}, bf16[2048,256]{1,0:T(8,128)(2,1)}, u32[]{:S(2)}) copy-start(bf16[2048,256]{1,0:T(8,128)(2,1)} %param.18) | copy-start | bytes 3145732
  7.2 65.3 %all-gather.10.cloned.1.call-start = ((), (), s32[]{:S(2)}) async-start(), calls=%async_computation.5 | async-start | bytes 4325376 | tf_op jit(solution)/shard_map/all_gather | solution.py:98
  7.9 125.6 %all-gather.6.cloned.1.call-start = ((), (), s32[]{:S(2)}) async-start(), calls=%async_computation.3 | async-start | bytes 4325376 | tf_op jit(solution)/shard_map/all_gather | solution.py:99
  9.8 164.0 %all-gather.12.cloned.1.call-start = ((), (), s32[]{:S(2)}) async-start(), calls=%async_computation.6 | async-start | bytes 1179648 | tf_op jit(solution)/shard_map/all_gather | solution.py:105
  77.9 95.9 %copy-start.2 = (f32[256,256]{1,0:T(8,128)S(1)}, f32[256,256]{1,0:T(8,128)}, u32[]{:S(2)}) copy-start(f32[256,256]{1,0:T(8,128)} %param.16) | copy-start | bytes 786436
  77.9 140.0 %all-gather.8.cloned.1.call-start = ((), (), s32[]{:S(2)}) async-start(), calls=%async_computation.4 | async-start | bytes 1179648 | tf_op jit(solution)/shard_map/all_gather | solution.py:106
  139.0 123.2 %reduce-scatter.3.cloned.1.call-start = ((), (), s32[]{:S(2)}) async-start(), calls=%async_computation.7 | async-start | bytes 1179648 | tf_op jit(solution)/shard_map/reduce_scatter | solution.py:118
  175.5 92.3 %copy-start.3 = (f32[256,256]{1,0:T(8,128)}, f32[256,256]{1,0:T(8,128)S(1)}, u32[]{:S(2)}) copy-start(f32[256,256]{1,0:T(8,128)S(1)} %fusion.14) | copy-start | bytes 786436
  221.5 144.5 %reduce-scatter.5.cloned.1.call-start = ((), (), s32[]{:S(2)}) async-start(), calls=%async_computation.8 | async-start | bytes 4325376 | tf_op jit(solution)/shard_map/reduce_scatter | solution.py:125
  267.8 0.7 copy-start.7
  267.8 6.9 %copy-start.4 = (f32[256,256]{1,0:T(8,128)S(1)}, f32[256,256]{1,0:T(8,128)}, u32[]{:S(2)}) copy-start(f32[256,256]{1,0:T(8,128)} %param.13) | copy-start | bytes 786436
  267.8 99.8 %copy-start.8 = (s32[4]{0:T(128)S(1)}, s32[4]{0:T(128)}, u32[]{:S(2)}) copy-start(s32[4]{0:T(128)} %param.25) | copy-start | bytes 52
  267.8 188.1 %copy-start.5 = (bf16[4,4,1024]{2,1,0:T(4,128)(2,1)S(1)}, bf16[4,4,1024]{2,1,0:T(4,128)(2,1)}, u32[]{:S(2)}) copy-start(bf16[4,4,1024]{2,1,0:T(4,128)(2,1)} %param.22) | copy-start | bytes 98308
  267.8 188.1 %copy-start.6 = (f32[8192]{0:T(1024)S(1)}, f32[8192]{0:T(1024)}, u32[]{:S(2)}) copy-start(f32[8192]{0:T(1024)} %param.20) | copy-start | bytes 98308
  267.8 188.2 %copy-start.1 = (bf16[4,1,512,128]{3,2,1,0:T(8,128)(2,1)S(1)}, bf16[4,1,512,128]{3,2,1,0:T(8,128)(2,1)}, u32[]{:S(2)}) copy-start(bf16[4,1,512,128]{3,2,1,0:T(8,128)(2,1)} %param.23) | copy-start | bytes 1572868
  267.9 178.2 %all-reduce.2.cloned.1.call-start = ((), (), s32[]{:S(2)}) async-start(), calls=%async_computation.9 | async-start | bytes 524288 | tf_op jit(solution)/shard_map/psum | solution.py:138
  274.6 236.7 %all-gather.14.cloned.1.call-start = ((), (), s32[]{:S(2)}) async-start(), calls=%async_computation.10 | async-start | bytes 4325376 | tf_op jit(solution)/shard_map/all_gather | solution.py:147
  446.1 23.4 %all-to-all-start = ((bf16[32,16,256]{2,1,0:T(8,128)(2,1)}), bf16[32,16,256]{2,1,0:T(8,128)(2,1)S(1)}, u32[]{:S(2)}, u32[]{:S(2)}) async-start(bf16[32,16,256]{2,1,0:T(8,128)(2,1)} %all-reduce.2.cloned.1.call-done), calls=%async_computation.2 | async-start | bytes 524288 | tf_op jit(solution)/shard_map/all_to_all | solution.py:141
  511.3 4.3 copy-start.9
Sparse Core Ops, SparseCore 0:
  10.6 61.8 all-gather.9
  75.6 57.8 all-gather.5
  135.3 38.5 all-gather.11
  176.0 41.8 all-gather.7
  221.6 40.6 reduce-scatter.2
  268.0 97.9 reduce-scatter.4
  369.4 76.6 all-reduce.1
  448.5 62.7 all-gather.13
where the time goes:
time: 528 us; the launch traced here: 524 us
  waiting for transfers between devices  459 us (87%)
  matrix products  26.2 us (5%)
  between operations  14.4 us (3%)
  starting transfers between devices  10.1 us (2%)
  local copies, waits for them, and re-layouts  8.55 us (2%)
  other arithmetic  5.3 us (1%)
    reduce_scatter x1, waiting for transfers between devices, shards(): lax.psum_scatter(contract_last(left_block, back_rows).astype(jnp.bfloat16...  91.2 us
    psum x1, waiting for transfers between devices, shards(): looked_up = lax.psum(picked.astype(jnp.float32).astype(jnp.bfloat16), 'tp')  78.3 us
    all_gather x1, waiting for transfers between devices, shards(): lax.all_gather(grad, 'fsdp', axis=0, tiled=True)  62.6 us
    all_gather x1, waiting for transfers between devices, shards(): lax.all_gather(moment_low, 'fsdp', axis=0, tiled=True)  55.6 us
    all_gather x1, waiting for transfers between devices, shards(): lax.all_gather(left_m.astype(jnp.bfloat16), 'tp', axis=1, tiled=True)  42.4 us
    reduce_scatter x1, waiting for transfers between devices, shards(): lax.psum_scatter(contract_last(right_block, direction).astype(jnp.bfloat1...  40.7 us
    all_gather x1, waiting for transfers between devices, shards(): lax.all_gather(weight, 'fsdp', axis=0, tiled=True)  39.6 us
    all_gather x1, waiting for transfers between devices, shards(): lax.all_gather(left_g.astype(jnp.bfloat16), 'tp', axis=1, tiled=True)  34.8 us
  transfers between devices with their start and end apart: 9, of which 9 were waited for; matrix products, arithmetic and copies ran while one was open for 5% of the time, Pallas kernels for 0%

commit v1 on v0

v1 whole, which is shorter than its diff:
```python
import functools

import jax
import jax.numpy as jnp
from jax import lax
from jax.experimental import pallas as pl
from jax.experimental.pallas import tpu as pltpu
from jax.sharding import Mesh, PartitionSpec as P

beta_one = 0.9
beta_two = 0.95
adam_eps = 1e-08
learn_rate = 0.003
adam_step = 20
norm_eps = 1e-06
rope_base = 1000000.0
token_unit = 2.0**-10

AXES = ("x", "zh", "c", "zl", "y")
SIZES = {"x": 4, "zh": 4, "c": 2, "zl": 2, "y": 4}
X, Z, C, L, Y = range(5)
f32 = jnp.float32
bf16 = jnp.bfloat16
VMEM_BYTES = 24 * 1024 * 1024


def call(body, outs, position, *args, far=(), deps=(), scratch=(), space=pltpu.VMEM):
    vmem = pl.BlockSpec(memory_space=pltpu.VMEM)
    return pl.pallas_call(
        body,
        out_shape=[jax.ShapeDtypeStruct(shape, kind) for shape, kind in outs],
        in_specs=[pl.BlockSpec(memory_space=pltpu.SMEM)]
        + [pl.BlockSpec(memory_space=pltpu.HBM)] * len(far)
        + [pl.BlockSpec(memory_space=pl.ANY)] * len(deps)
        + [vmem] * len(args),
        out_specs=[pl.BlockSpec(memory_space=space)] * len(outs),
        scratch_shapes=list(scratch),
        compiler_params=pltpu.CompilerParams(vmem_limit_bytes=VMEM_BYTES),
    )(position, *far, *deps, *args)


def shift(array, axis, by):
    size = SIZES[axis]
    return lax.ppermute(array, axis, [(i, (i + by) % size) for i in range(size)])


def swap(array):
    return shift(array, "c", 1)


def others(array, axis):
    return [shift(array, axis, k) for k in range(1, SIZES[axis])]


def scatter(arrays, axis):
    return [shift(array, axis, -k) for k, array in enumerate(arrays) if k]


def dot(left, right, left_dim=1, right_dim=0):
    return lax.dot_general(
        left, right, (((left_dim,), (right_dim,)), ((), ())), preferred_element_type=f32
    )


def chip_place(pos, i, j):
    return ((pos[X] + 4 - i) % 4) * 4 + (pos[Z] + 4 - j) % 4


def turn_body(array, out):
    out[...] = array[...].astype(f32).T.astype(bf16)


def moment_body(pos, grad, moment, master, moment_new, turned, low):
    new = beta_one * moment[...] + (1.0 - beta_one) * grad[...].astype(f32)
    moment_new[...] = new
    turned[...] = new.astype(bf16).astype(f32).T.astype(bf16)
    low[...] = master[...].astype(bf16)


def moment_tokens_body(pos, turned, arrived, owner, out):
    cols = turned.shape[0]
    out[:cols, :] = turned[...]
    total = None
    for i in range(8):
        part = jnp.where(owner[...] == i, arrived[i].astype(f32), 0.0)
        total = part if total is None else total + part
    out[cols:, :] = total.astype(bf16)


def wide_body(pos, *refs):
    out = refs[-1]
    for i, piece in enumerate(refs[-5:-1]):
        out[:, i * piece.shape[1] : (i + 1) * piece.shape[1]] = piece[...]


def basis_body(pos, own, other, out, sems):
    size = out.shape[1] // 2

    def copies(n):
        place = pl.multiple_of((chip_place(pos, n // 4, n % 4) * 2 + pos[C]) * size, size)
        slot = pl.ds(pl.multiple_of(n * size, size), size)
        return [
            pltpu.make_async_copy(
                ref.at[pl.ds(place, size), :], out.at[slot, pl.ds(k * size, size)], sems.at[n, k]
            )
            for k, ref in enumerate((own, other))
        ]

    def start(n, carry):
        for copy in copies(n):
            copy.start()
        return carry

    def wait(n, carry):
        for copy in copies(n):
            copy.wait()
        return carry

    lax.fori_loop(0, 16, start, 0)
    lax.fori_loop(0, 16, wait, 0)


def basis_parts(basis, buf, sems, order):
    deep = buf.shape[0] // 4
    copies = {}
    for i in order:
        part = pl.ds(i * deep, deep)
        copies[i] = pltpu.make_async_copy(basis.at[part, :], buf.at[part, :], sems.at[i])
        copies[i].start()

    def read(i):
        copies[i].wait()
        return buf[i * deep : (i + 1) * deep, :]

    return read


def left_body(pos, basis, dep, p0, p1, top, low, p3, keep, send, buf, sems):
    size = keep.shape[1]
    read = basis_parts(basis, buf, sems, (0, 1, 3, 2))
    total = None
    for i, piece in ((0, p0[...]), (1, p1[...]), (3, p3[...]), (2, None)):
        if piece is None:
            piece = jnp.concatenate([top[...], low[...]], 0)
        part = dot(piece, read(i))
        total = part if total is None else total + part
    keep[...] = total[:, :size]
    send[...] = total[:, size:]


def left_tokens_body(
    pos, basis, dep, gain, p0, p1, top, low, p3, keep, send, buf, sems, turned, first, square
):
    cols = size = send.shape[1]
    read = basis_parts(basis, buf, sems, (0, 1, 3, 2))
    n_tok = p0.shape[0] - cols
    squares = 0.0
    total = None
    for i, piece in ((0, p0[...]), (1, p1[...]), (3, p3[...]), (2, None)):
        if piece is None:
            piece = jnp.concatenate([top[...], low[...]], 0)
        gains = jnp.concatenate([gain[chip_place(pos, i, j) * 2 + pos[C]] for j in range(4)], -1)
        feats = piece[cols:, :].astype(f32)
        squares = squares + jnp.sum(feats * feats, -1, keepdims=True)
        feats = feats * gains * token_unit
        if i == 0:
            first[...] = feats[:, :size].reshape(first.shape)
        piece = jnp.concatenate([piece[:cols, :], feats.astype(bf16)], 0)
        part = dot(piece, read(i))
        total = part if total is None else total + part
    keep[:cols, :] = total[:cols, :size]
    send[:cols, :] = total[:cols, size:]
    for k in range(2):
        turned[k] = total[cols:, k * size : (k + 1) * size].reshape(2, n_tok // 2, size)
    square[...] = jnp.broadcast_to(squares, (n_tok, size)).reshape(square.shape)
    rows = n_tok // 2
    core = pos[C]
    for out, which, order in ((keep, core, (1, 0)), (send, 1 - core, (0, 1))):
        at = cols
        for value in (turned[order[0], which], turned[order[1], which], first[which], square[which]):
            out[at : at + rows, :] = value
            at += rows


def left_sum_body(pos, keep, recv, out):
    out[...] = (keep[...] + recv[...]).T.astype(bf16)


def pair_body(pos, here, there, out):
    out[0] = here[...]
    out[1] = there[...]


def left_tokens_sum_body(pos, keep, recv, all_out, out):
    cols = keep.shape[1]
    rows = (out.shape[0] - cols) // 4
    out[:cols, :] = (keep[:cols, :] + recv[:cols, :]).T.astype(bf16)
    parts = [slice(cols + k * rows, cols + (k + 1) * rows) for k in range(4)]
    square = keep[parts[3], :] + recv[parts[3], :]
    scale = lax.rsqrt(square / (32 * cols) + norm_eps) * (1.0 / token_unit)
    turned_other = keep[parts[0], :] + recv[parts[0], :]
    turned_own = keep[parts[1], :] + recv[parts[1], :]
    values = (
        keep[parts[2], :] * scale,
        recv[parts[2], :] * scale,
        turned_own * scale * (-learn_rate),
        turned_other * scale * (-learn_rate),
    )
    for part, value in zip(parts, values):
        out[part, :] = value.astype(bf16)
    for n in range(8):
        all_out[n] = out[...]


def variance_body(pos, right, variance, s0, s1, s2, s3, out):
    cols = right.shape[1]
    rot = None
    for j, piece in enumerate((s0, s1, s2, s3)):
        for i in range(2):
            place = ((pos[L] + 2 - i) % 2) * 4 + (pos[Y] + 4 - j) % 4
            rows = pl.ds(pl.multiple_of(place * cols, cols), cols)
            part = dot(piece[i], right[rows, :])
            rot = part if rot is None else rot + part
    out[...] = beta_two * variance[...] + (1.0 - beta_two) * rot * rot


def direction_body(pos, right, variance_new, left, out):
    cols = right.shape[1]
    rot = None
    for n in range(8):
        part = dot(left[n, :cols, :], right[n * cols : (n + 1) * cols, :])
        rot = part if rot is None else rot + part
    corr_one = 1.0 - beta_one**adam_step
    corr_two = 1.0 - beta_two**adam_step
    value = rot / corr_one / (jnp.sqrt(variance_new[...] / corr_two) + adam_eps)
    value = value.astype(bf16)
    for n in range(8):
        out[n] = dot(value, right[n * cols : (n + 1) * cols, :], 1, 1).astype(bf16)


def back_body(pos, parts, out):
    out[...] = sum(parts[n].astype(f32) for n in range(8)).astype(bf16)


def update_far_body(pos, basis, back_own, back_other, kv, top, low, buf, sems, whole):
    update_body((2,), pos, basis, back_own, back_other, kv, whole, buf, sems)
    half = top.shape[0]
    top[...] = whole[:half, :]
    low[...] = whole[half:, :]


def add_halves_body(pos, one, three, top, low, o1, o3):
    half = top.shape[0]
    o1[:half, :] = (one[:half, :].astype(f32) + top[...].astype(f32)).astype(bf16)
    o1[half:, :] = one[half:, :]
    o3[:half, :] = three[:half, :]
    o3[half:, :] = (three[half:, :].astype(f32) + low[...].astype(f32)).astype(bf16)


def update_body(steps, pos, basis, back_own, back_other, kv, *refs):
    size = back_own.shape[0]
    rows = kv.shape[2]
    back = jnp.concatenate([back_own[...], back_other[...]], 0)
    read = basis_parts(basis, refs[-2], refs[-1], steps)
    for i, out in zip(steps, refs):
        part = read(i)
        for n in range(0, 4, 2):
            rows_here = slice(n * size, (n + 2) * size)
            out[rows_here, :] = dot(part[rows_here, :], back).astype(bf16)
        for j in range(4):
            out[4 * size + j * rows : 4 * size + (j + 1) * rows, :] = kv[i, j]


def kv_body(pos, w_own, w_other, b_own, b_other, left, total):
    size = w_own.shape[0]
    many = (left.shape[1] - size) // 4
    rows = many // 2
    value = None
    for k, ref in enumerate((w_own, w_other, b_own, b_other)):
        part = slice(size + k * many, size + (k + 1) * many)
        part = dot(jnp.concatenate([left[n, part, :] for n in range(8)], 0), ref[...])
        value = part if value is None else value + part
    for n in range(8):
        step_x = (pos[X] + 4 - n % 4) % 4
        for low in range(2):
            step_z = (pos[Z] + 4 - (n // 4) * 2 - low) % 4
            first = (2 * n + low) * rows
            total[step_x, step_z] = value[first : first + rows].astype(bf16)


def sums_body(pos, a, b, c, keep, o1, o2, o3):
    rows = o1.shape[0] - o1.shape[1]
    size = o1.shape[0] - rows
    refs = (a, b, c)
    for j, out in enumerate((keep, o1, o2, o3)):
        for to, at, many in ((0, j * size, size), (size, 4 * size + j * rows, rows)):
            total = sum(ref[at : at + many, :].astype(f32) for ref in refs)
            out[to : to + many, :] = total.astype(out.dtype)


def attend_old_body(pos, dep, query, keys, values, out, row_max, row_sum):
    seqs, rows, head_dim = query.shape
    scaling = float(head_dim) ** (-0.5)
    cells = lax.broadcasted_iota(jnp.int32, (rows, keys.shape[1]), 1)
    for s in range(seqs):
        score = dot(query[s], keys[s], 1, 1) * scaling
        inside = cells < pos[len(AXES) + s]
        score = jnp.where(inside, score, -1e30)
        top = jnp.max(score, -1, keepdims=True)
        value = jnp.where(inside, jnp.exp(score - top), 0.0)
        out[s] = dot(value.astype(bf16), values[s])
        row_max[s] = jnp.broadcast_to(top, (rows, head_dim))
        row_sum[s] = jnp.broadcast_to(jnp.sum(value, -1, keepdims=True), (rows, head_dim))


def finish_body(
    pos, kept, one, two, three, cosine, sine_part, query, old, row_max, row_sum, update, out, stage
):
    size = update.shape[0]
    total = kept[...] + sum(ref[...].astype(f32) for ref in (one, two, three))
    update[...] = total[:size]
    total = total[size:]
    steps = out.shape[1]
    seqs, rows, head_dim = query.shape
    scaling = float(head_dim) ** (-0.5)
    count = total.shape[0]
    keys = total[:, :head_dim]
    values = total[:, head_dim:].astype(bf16)
    half = head_dim // 2
    turned = jnp.concatenate([keys[:, half:], keys[:, :half]], 1)
    keys = (keys * cosine[...] + turned * sine_part[...]).astype(bf16)
    cells = lax.broadcasted_iota(jnp.int32, (rows, count), 1)
    row_ids = lax.broadcasted_iota(jnp.int32, (rows, count), 0)
    query_step = sum((row_ids >= t * (rows // steps)).astype(jnp.int32) for t in range(1, steps))
    for s in range(seqs):
        score = dot(query[s], keys, 1, 1) * scaling
        inside = (cells >= s * steps) & (cells <= s * steps + query_step)
        score = jnp.where(inside, score, -1e30)
        top = row_max[s]
        new_top = jnp.maximum(top, jnp.max(score, -1, keepdims=True))
        shrink = jnp.exp(top - new_top)
        value = jnp.where(inside, jnp.exp(score - new_top[:, :1]), 0.0)
        sums = row_sum[s] * shrink + jnp.sum(value, -1, keepdims=True)
        stage[...] = (old[s] * shrink + dot(value.astype(bf16), values)) / sums
        group = rows // steps
        for g in range(group):
            out[s, :, g * head_dim : (g + 1) * head_dim] = stage[g::group, :]


def exchange(array):
    return lax.all_to_all(array, ("zl", "y"), 0, 0, tiled=True)


def ring_first(array):
    half = array.shape[0] // 2
    one, three = shift(array, "x", 1), shift(array, "x", -1)
    return one, three, one[:half], three[half:]


def ring_gather(array, first):
    one, three, top, low = first
    return [array, one, shift(top, "x", 1), shift(low, "x", -1), three]


def after(array, *deps):
    return lax.optimization_barrier((array,) + deps)[0]


def shards(
    master,
    grad,
    moment,
    variance,
    q_left,
    q_right,
    embed,
    gain,
    token_ids,
    queries,
    k_cache,
    v_cache,
    cache_len,
):
    axis_places = jnp.stack([lax.axis_index(name) for name in AXES]).astype(jnp.int32)
    position = jnp.concatenate([axis_places, cache_len])
    group_at = lax.axis_index(("zl", "y"))
    rows, cols = grad.shape
    square = (rows, cols)

    grad_t = pl.pallas_call(
        turn_body,
        out_shape=jax.ShapeDtypeStruct((cols, rows), bf16),
        compiler_params=pltpu.CompilerParams(vmem_limit_bytes=VMEM_BYTES),
    )(grad)
    grad_z = others(grad_t, "zh")

    flat_ids = token_ids.reshape(4, 2, 2, 2, -1)
    tok_rows = flat_ids.shape[-1]
    flat_ids = after(jnp.transpose(flat_ids, (1, 0, 3, 2, 4)).reshape(-1), grad_z[0])
    n_tok = flat_ids.shape[0]
    vocab_rows = embed.shape[0]
    local_ids = jnp.clip(flat_ids - group_at * vocab_rows, 0, vocab_rows - 1)
    picked = embed.at[local_ids].get(mode="promise_in_bounds").reshape(8, n_tok // 8, rows)
    arrived = exchange(picked)
    owner = (flat_ids // vocab_rows).reshape(8, n_tok // 8)
    owner = lax.dynamic_index_in_dim(owner, group_at, 0, keepdims=False).reshape(-1, 1)

    q_other = swap(after(q_left, grad_t))
    (basis,) = call(
        basis_body,
        [((16 * rows, 2 * rows), bf16)],
        position,
        far=(q_left, q_other),
        scratch=[pltpu.SemaphoreType.DMA((16, 2))],
        space=pltpu.HBM,
    )
    basis_scratch = [pltpu.VMEM(basis.shape, bf16), pltpu.SemaphoreType.DMA((4,))]
    moment_new, moment_t, master_low = call(
        moment_body,
        [(square, f32), ((cols, rows), bf16), (square, bf16)],
        position,
        after(grad, grad_t),
        moment,
        master,
    )
    deep = cols + n_tok // 8
    (grad_x,) = call(wide_body, [((cols, 4 * rows), bf16)], position, grad_t, *grad_z, deps=(picked, q_other))
    grad_first = ring_first(grad_x)
    grad_pieces = ring_gather(grad_x, grad_first)
    (moment_z,) = call(
        moment_tokens_body,
        [((deep, rows), bf16)],
        position,
        moment_t,
        arrived,
        owner,
    )
    moment_z = after(moment_z, grad_x)
    moment_others = others(moment_z, "zh")
    (moment_x,) = call(
        wide_body, [((deep, 4 * rows), bf16)], position, moment_z, *moment_others, deps=(*grad_pieces[2:4], basis)
    )
    moment_first = ring_first(moment_x)
    moment_pieces = ring_gather(moment_x, moment_first)

    master_other = swap(master_low)

    seqs, steps = queries.shape[0], queries.shape[1]
    head_dim = k_cache.shape[-1]
    query_rows = queries.reshape(seqs, -1, head_dim)
    old_out, old_max, old_sum = call(
        attend_old_body,
        [(query_rows.shape, f32)] * 3,
        position,
        query_rows,
        k_cache.reshape(seqs, -1, head_dim),
        v_cache.reshape(seqs, -1, head_dim),
        deps=(moment_others[0],),
    )
    token_at = (cache_len[:, None] + jnp.arange(steps, dtype=jnp.int32)[None, :]).reshape(-1, 1)
    inverse = rope_base ** (-(jnp.arange(head_dim // 2, dtype=f32) * 2.0 / head_dim))
    angles = after(token_at, moment_others[0]).astype(f32) * inverse
    cosine = jnp.concatenate([jnp.cos(angles)] * 2, 1)
    sine_part = jnp.concatenate([-jnp.sin(angles), jnp.sin(angles)], 1)

    keep, send = call(
        left_body,
        [((cols, rows), f32)] * 2,
        position,
        *grad_pieces,
        far=(basis,),
        deps=(moment_x,),
        scratch=basis_scratch,
    )
    (left_g,) = call(left_sum_body, [(square, bf16)], position, keep, swap(send))
    (left_g,) = call(
        pair_body, [((2,) + square, bf16)], position, left_g, shift(left_g, "zl", 1)
    )
    (variance_new,) = call(
        variance_body, [(square, f32)], position, q_right, variance, left_g, *others(left_g, "y")
    )

    keep, send = call(
        left_tokens_body,
        [((cols + n_tok // 4, rows), f32)] * 2,
        position,
        gain.reshape(32, 1, rows),
        *moment_pieces,
        far=(basis,),
        deps=(variance_new,),
        scratch=basis_scratch
        + [
            pltpu.VMEM((2, 2, n_tok // 16, rows), f32),
            pltpu.VMEM((2, n_tok // 16, rows), f32),
            pltpu.VMEM((2, n_tok // 16, rows), f32),
        ],
    )
    (left_m,) = call(
        left_tokens_sum_body,
        [((8, cols + n_tok // 4, rows), bf16)],
        position,
        keep,
        swap(send),
        scratch=[pltpu.VMEM((cols + n_tok // 4, rows), bf16)],
    )
    left_m = exchange(left_m)

    (parts,) = call(
        direction_body, [((8,) + square, bf16)], position, q_right, variance_new, left_m
    )
    (back_own,) = call(back_body, [(square, bf16)], position, exchange(parts))
    back_other = swap(back_own)

    (kv,) = call(
        kv_body,
        [((4, 4, tok_rows, cols), bf16)],
        position,
        master_low,
        master_other,
        back_own,
        back_other,
        left_m,
    )

    many = 4 * (rows + tok_rows)
    top, low = call(
        update_far_body,
        [((many // 2, cols), bf16)] * 2,
        position,
        back_own,
        back_other,
        kv,
        far=(basis,),
        scratch=basis_scratch + [pltpu.VMEM((many, cols), bf16)],
    )
    top, low = shift(top, "x", -1), shift(low, "x", 1)
    one, three, zero = call(
        functools.partial(update_body, (1, 3, 0)),
        [((many, cols), bf16)] * 3,
        position,
        back_own,
        back_other,
        kv,
        far=(basis,),
        scratch=basis_scratch,
    )
    one, three = call(
        add_halves_body, [((many, cols), bf16)] * 2, position, one, three, top, low
    )
    parts = call(
        sums_body,
        [((rows + tok_rows, cols), f32)] + [((rows + tok_rows, cols), bf16)] * 3,
        position,
        zero,
        shift(one, "x", -1),
        shift(three, "x", 1),
    )
    update, attended = call(
        finish_body,
        [(square, f32), (queries.shape, f32)],
        position,
        parts[0],
        *scatter(parts, "zh"),
        cosine,
        sine_part,
        query_rows,
        old_out,
        old_max,
        old_sum,
        scratch=[pltpu.VMEM(query_rows.shape[1:], f32)],
    )
    return (update, moment_new, variance_new, attended)


def solution(mesh):
    fine = Mesh(mesh.devices.reshape([SIZES[name] for name in AXES]), AXES)
    fsdp = ("x", "zh", "c")
    tp = ("zl", "y")
    in_specs = (
        P(fsdp, tp),
        P(fsdp, tp),
        P(fsdp, tp),
        P(fsdp, tp),
        P(None, fsdp),
        P(None, tp),
        P(tp, fsdp),
        P(),
        P(),
        P(fsdp, None, tp),
        P(fsdp, tp, None, None),
        P(fsdp, tp, None, None),
        P(fsdp),
    )
    out_specs = (P(fsdp, tp), P(fsdp, tp), P(fsdp, tp), P(fsdp, None, tp))
    return jax.shard_map(shards, mesh=fine, in_specs=in_specs, out_specs=out_specs, check_vma=False)
```

time: 528 us -> 207 us (0.39)
  waiting for transfers between devices: 459 us -> 82.7 us
  starting transfers between devices: 10.1 us -> 57.4 us
  Pallas kernels: 0 us -> 27.4 us
  matrix products: 26.2 us -> 0 us
  blocking collectives: 0 us -> 23.3 us
  between operations: 14.4 us -> 1.09 us
  local copies, waits for them, and re-layouts: 8.55 us -> 14.6 us
    all_gather x5 -> x0, waiting for transfers between devices: 235 us -> none  [the longest x1 62.6 us: shards(): lax.all_gather(grad, 'fsdp', axis=0, tiled=True)]
    reduce_scatter x2 -> x0, waiting for transfers between devices: 132 us -> none  [the longest x1 91.2 us: shards(): lax.psum_scatter(contract_last(left_block, back_rows).astype(jnp.bfloat16...]
    psum x1 -> x0, waiting for transfers between devices: 78.3 us -> none  [shards(): looked_up = lax.psum(picked.astype(jnp.float32).astype(jnp.bfloat16), 'tp')]
    ppermute x0 -> x30, waiting for transfers between devices: none -> 69.5 us  [shift(): lax.ppermute(array, axis, [(i, (i + by) % size) for i in range(size)])]
    ppermute x0 -> x30, starting transfers between devices: none -> 46.6 us  [shift(): lax.ppermute(array, axis, [(i, (i + by) % size) for i in range(size)])]
    pallas_call x0 -> x21, Pallas kernels: none -> 27.4 us  [the longest x20 27.3 us: call(): pl.pallas_call(body, out_shape=[jax.ShapeDtypeStruct(shape, kind) for sha...]
    dot_general x10 -> x0, matrix products: 26.2 us -> none  [the longest x2 10.8 us: contract_first(): lax.dot_general(left_op, right_op, (((0,), (0,)), ((), ())), preferred_el...]
    all_to_all x0 -> x1, blocking collectives: none -> 23.3 us  [exchange(): return lax.all_to_all(array, ('zl', 'y'), 0, 0, tiled=True)]
  transfers between devices with their start and end apart: 9 -> 32, of which waited for: 9 -> 20; matrix products, arithmetic and copies ran while one was open for 5% -> 4% of each run, Pallas kernels for 0% -> 7%
where the time goes in v1:
time: 207 us
  waiting for transfers between devices  82.7 us (40%)
  starting transfers between devices  57.4 us (28%)
  Pallas kernels  27.4 us (13%)
  blocking collectives  23.3 us (11%)
  local copies, waits for them, and re-layouts  14.6 us (7%)
    ppermute x30, waiting for transfers between devices, shift(): lax.ppermute(array, axis, [(i, (i + by) % size) for i in range(size)])  69.5 us
    ppermute x30, starting transfers between devices, shift(): lax.ppermute(array, axis, [(i, (i + by) % size) for i in range(size)])  46.6 us
    pallas_call x20, Pallas kernels, call(): pl.pallas_call(body, out_shape=[jax.ShapeDtypeStruct(shape, kind) for sha...  27.3 us
    all_to_all x1, blocking collectives, exchange(): return lax.all_to_all(array, ('zl', 'y'), 0, 0, tiled=True)  23.3 us
    all_to_all x2, waiting for transfers between devices, exchange(): return lax.all_to_all(array, ('zl', 'y'), 0, 0, tiled=True)  13.1 us
    all_to_all x2, starting transfers between devices, exchange(): return lax.all_to_all(array, ('zl', 'y'), 0, 0, tiled=True)  10.8 us
    unnamed x33, local copies, waits for them, and re-layouts  8.07 us
    gather x1, local copies, waits for them, and re-layouts, shards(): embed.at[local_ids].get(mode='promise_in_bounds')  5.27 us
  transfers between devices with their start and end apart: 32, of which 20 were waited for; matrix products, arithmetic and copies ran while one was open for 4% of the time, Pallas kernels for 7%

profile of v1, /device:TPU:32, one launch (start us, length us, event | category | flops | bytes accessed | tf_op | source)
XLA Modules:
  0.0 206.8 jit_solution(16189447864342515194)
XLA Ops:
  1.7 3.3 %collective-permute-start.1 = (bf16[256,256]{1,0:T(8,128)(2,1)S(1)}, bf16[256,256]{1,0:T(8,128)(2,1)S(1)}, u32[]{:S(2)}, u32[]{:S(2)}) collective-permute-start(bf16[256,256]{1,0:T(8,128)(2,1)S(1)} %shard_map.156.refs_2_), channel_id=1, source_target_pairs={{0,16},{16,32},{32,48},{48,0},{1,17},{17,33},{33,49},{49,1},{2,18}... | collective-permute-start | bytes 393224 | tf_op jit(solution)/shard_map/ppermute | solution.py:44
  7.3 4.9 %collective-permute-start.2 = (bf16[256,256]{1,0:T(8,128)(2,1)S(1)}, bf16[256,256]{1,0:T(8,128)(2,1)S(1)}, u32[]{:S(2)}, u32[]{:S(2)}) collective-permute-start(bf16[256,256]{1,0:T(8,128)(2,1)S(1)} %shard_map.156.refs_2_), channel_id=1, source_target_pairs={{0,32},{16,48},{32,0},{48,16},{1,33},{17,49},{33,1},{49,17},{2,34}... | collective-permute-start | bytes 393224 | tf_op jit(solution)/shard_map/ppermute | solution.py:44
  14.9 5.3 %gather_fusion = bf16[512,256]{1,0:T(8,128)(2,1)} fusion(bf16[9504,256]{1,0:T(8,128)(2,1)} %param.19, s32[1024]{0:T(1024)S(1)} %pad_clamp_fusion), kind=kCustom, calls=%fused_computation | custom fusion | bytes 526336 | tf_op jit(solution)/shard_map/gather | solution.py:403
  20.2 3.5 %collective-permute-done.2.refs_4_ = bf16[256,256]{1,0:T(8,128)(2,1)S(1)} collective-permute-done((bf16[256,256]{1,0:T(8,128)(2,1)S(1)}, bf16[256,256]{1,0:T(8,128)(2,1)S(1)}, u32[]{:S(2)}, u32[]{:S(2)}) %collective-permute-start.2) | collective-permute-done | bytes 131104 | tf_op jit(solution)/shard_map/ppermute | solution.py:44
  27.1 5.9 %all-to-all-start = ((bf16[8,64,256]{2,1,0:T(8,128)(2,1)}), bf16[8,64,256]{2,1,0:T(8,128)(2,1)S(1)}, u32[]{:S(2)}, u32[]{:S(2)}) async-start(bf16[8,64,256]{2,1,0:T(8,128)(2,1)} %bitcast.6.refs_0_), calls=%async_computation | async-start | bytes 524288 | tf_op jit(solution)/shard_map/all_to_all | solution.py:351
  34.4 3.7 %collective-permute-done.6.p3 = bf16[256,1024]{1,0:T(8,128)(2,1)S(1)} collective-permute-done((bf16[256,1024]{1,0:T(8,128)(2,1)S(1)}, bf16[256,1024]{1,0:T(8,128)(2,1)S(1)}, u32[]{:S(2)}, u32[]{:S(2)}) %collective-permute-start.6) | collective-permute-done | bytes 524320 | tf_op jit(solution)/shard_map/ppermute | solution.py:44
  38.1 3.8 %collective-permute-start.7 = (bf16[128,1024]{1,0:T(8,128)(2,1)S(1)}, bf16[128,1024]{1,0:T(8,128)(2,1)S(1)}, u32[]{:S(2)}, u32[]{:S(2)}) collective-permute-start(bf16[128,1024]{1,0:T(8,128)(2,1)S(1)} %slice.19), channel_id=1, source_target_pairs={{0,192},{64,0},{128,64},{192,128},{1,193},{65,1},{129,65},{193,129... | collective-permute-start | bytes 786440 | tf_op jit(solution)/shard_map/ppermute | solution.py:44
  53.1 3.9 %collective-permute-done.9.refs_5_ = bf16[320,256]{1,0:T(8,128)(2,1)S(1)} collective-permute-done((bf16[320,256]{1,0:T(8,128)(2,1)S(1)}, bf16[320,256]{1,0:T(8,128)(2,1)S(1)}, u32[]{:S(2)}, u32[]{:S(2)}) %collective-permute-start.9) | collective-permute-done | bytes 163872 | tf_op jit(solution)/shard_map/ppermute | solution.py:44
  60.1 3.0 %collective-permute-start.18 = (bf16[320,1024]{1,0:T(8,128)(2,1)S(1)}, bf16[320,1024]{1,0:T(8,128)(2,1)S(1)}, u32[]{:S(2)}, u32[]{:S(2)}) collective-permute-start(bf16[320,1024]{1,0:T(8,128)(2,1)S(1)} %shard_map.161.dep.p0), channel_id=1, source_target_pairs={{0,192},{64,0},{128,64},{192,128},{1,193},{65,1},{129,65},{193,129... | collective-permute-start | bytes 1966088 | tf_op jit(solution)/shard_map/ppermute | solution.py:44
  67.9 9.4 %collective-permute-done.18.p3 = bf16[320,1024]{1,0:T(8,128)(2,1)S(1)} collective-permute-done((bf16[320,1024]{1,0:T(8,128)(2,1)S(1)}, bf16[320,1024]{1,0:T(8,128)(2,1)S(1)}, u32[]{:S(2)}, u32[]{:S(2)}) %collective-permute-start.18) | collective-permute-done | bytes 655392 | tf_op jit(solution)/shard_map/ppermute | solution.py:44
  77.3 3.8 %collective-permute-start.19 = (bf16[160,1024]{1,0:T(8,128)(2,1)S(1)}, bf16[160,1024]{1,0:T(8,128)(2,1)S(1)}, u32[]{:S(2)}, u32[]{:S(2)}) collective-permute-start(bf16[160,1024]{1,0:T(8,128)(2,1)S(1)} %slice.21), channel_id=1, source_target_pairs={{0,192},{64,0},{128,64},{192,128},{1,193},{65,1},{129,65},{193,129... | collective-permute-start | bytes 983048 | tf_op jit(solution)/shard_map/ppermute | solution.py:44
  81.8 3.1 %collective-permute-start.15 = (bf16[2,256,256]{2,1,0:T(8,128)(2,1)S(1)}, bf16[2,256,256]{2,1,0:T(8,128)(2,1)S(1)}, u32[]{:S(2)}, u32[]{:S(2)}) collective-permute-start(bf16[2,256,256]{2,1,0:T(8,128)(2,1)S(1)} %shard_map.164.s0), channel_id=1, source_target_pairs={{0,3},{1,0},{2,1},{3,2},{4,7},{5,4},{6,5},{7,6},{8,11},{9,8},{10,9... | collective-permute-start | bytes 786440 | tf_op jit(solution)/shard_map/ppermute | solution.py:44
  86.5 8.6 %collective-permute-done.15.s3 = bf16[2,256,256]{2,1,0:T(8,128)(2,1)S(1)} collective-permute-done((bf16[2,256,256]{2,1,0:T(8,128)(2,1)S(1)}, bf16[2,256,256]{2,1,0:T(8,128)(2,1)S(1)}, u32[]{:S(2)}, u32[]{:S(2)}) %collective-permute-start.15) | collective-permute-done | bytes 262176 | tf_op jit(solution)/shard_map/ppermute | solution.py:44
  95.6 3.2 %collective-permute-done.13.s1 = bf16[2,256,256]{2,1,0:T(8,128)(2,1)S(1)} collective-permute-done((bf16[2,256,256]{2,1,0:T(8,128)(2,1)S(1)}, bf16[2,256,256]{2,1,0:T(8,128)(2,1)S(1)}, u32[]{:S(2)}, u32[]{:S(2)}) %collective-permute-start.13) | collective-permute-done | bytes 262176 | tf_op jit(solution)/shard_map/ppermute | solution.py:44
  101.5 2.9 %shard_map.166 = (f32[384,256]{1,0:T(8,128)S(1)}, f32[384,256]{1,0:T(8,128)S(1)}) custom-call(s32[9]{0:T(128)S(1)} %concatenate.9.pos, bf16[4096,512]{1,0:T(8,128)(2,1)S(1)} %shard_map.157.refs_2_.basis, f32[256,256]{1,0:T(8,128)S(1)} %copy-done.5, f32[32,1,256]{2,1,0:T(1,128)S(1)} %bitcast.16, bf16[320,1024]{1,0:T(8,128)(2,1)S(1)} %shard_map.161.dep.p0, ...), custom_call_target="tpu_custom_call" | custom-call | tf_op jit(solution)/shard_map/pallas_call | solution.py:29
  106.9 23.3 %all_to_all.15.left = bf16[8,384,256]{2,1,0:T(8,128)(2,1)S(1)} all-to-all(bf16[8,384,256]{2,1,0:T(8,128)(2,1)S(1)} %shard_map.167), channel_id=1, replica_groups=mesh['x'=4,'zh'=4,'c'=2,'zl'=2,'y'=4] {'zl','y'}, dimensions={0} | all-to-all | bytes 3145728 | tf_op jit(solution)/shard_map/all_to_all | solution.py:351
  133.1 4.9 %all-to-all-start.2 = ((bf16[8,256,256]{2,1,0:T(8,128)(2,1)}), bf16[8,256,256]{2,1,0:T(8,128)(2,1)S(1)}, u32[]{:S(2)}, u32[]{:S(2)}) async-start(bf16[8,256,256]{2,1,0:T(8,128)(2,1)} %copy-done.4), calls=%async_computation.2 | async-start | bytes 2097152 | tf_op jit(solution)/shard_map/all_to_all | solution.py:351
  138.0 13.1 %all-to-all-done.2.parts = bf16[8,256,256]{2,1,0:T(8,128)(2,1)S(1)} async-done(((bf16[8,256,256]{2,1,0:T(8,128)(2,1)}), bf16[8,256,256]{2,1,0:T(8,128)(2,1)S(1)}, u32[]{:S(2)}, u32[]{:S(2)}) %all-to-all-start.2) | async-done | bytes 1048608 | tf_op jit(solution)/shard_map/all_to_all | solution.py:351
  157.4 3.0 %collective-permute-start.23 = (bf16[544,256]{1,0:T(8,128)(2,1)S(1)}, bf16[544,256]{1,0:T(8,128)(2,1)S(1)}, u32[]{:S(2)}, u32[]{:S(2)}) collective-permute-start(bf16[544,256]{1,0:T(8,128)(2,1)S(1)} %get-tuple-element.45), channel_id=1, source_target_pairs={{0,192},{64,0},{128,64},{192,128},{1,193},{65,1},{129,65},{193,129... | collective-permute-start | bytes 835592 | tf_op jit(solution)/shard_map/ppermute | solution.py:44
  162.6 4.1 %collective-permute-done.23.top = bf16[544,256]{1,0:T(8,128)(2,1)S(1)} collective-permute-done((bf16[544,256]{1,0:T(8,128)(2,1)S(1)}, bf16[544,256]{1,0:T(8,128)(2,1)S(1)}, u32[]{:S(2)}, u32[]{:S(2)}) %collective-permute-start.23) | collective-permute-done | bytes 278560 | tf_op jit(solution)/shard_map/ppermute | solution.py:44
  166.7 3.4 %collective-permute-done.24.low = bf16[544,256]{1,0:T(8,128)(2,1)S(1)} collective-permute-done((bf16[544,256]{1,0:T(8,128)(2,1)S(1)}, bf16[544,256]{1,0:T(8,128)(2,1)S(1)}, u32[]{:S(2)}, u32[]{:S(2)}) %collective-permute-start.24) | collective-permute-done | bytes 278560 | tf_op jit(solution)/shard_map/ppermute | solution.py:44
  174.0 11.5 %collective-permute-done.25.b = bf16[1088,256]{1,0:T(8,128)(2,1)S(1)} collective-permute-done((bf16[1088,256]{1,0:T(8,128)(2,1)}, bf16[1088,256]{1,0:T(8,128)(2,1)S(1)}, u32[]{:S(2)}, u32[]{:S(2)}) %collective-permute-start.25) | collective-permute-done | bytes 557088 | tf_op jit(solution)/shard_map/ppermute | solution.py:44
  187.8 4.0 %collective-permute-start.27 = (bf16[272,256]{1,0:T(8,128)(2,1)S(1)}, bf16[272,256]{1,0:T(8,128)(2,1)S(1)}, u32[]{:S(2)}, u32[]{:S(2)}) collective-permute-start(bf16[272,256]{1,0:T(8,128)(2,1)S(1)} %get-tuple-element.50), channel_id=1, source_target_pairs={{0,48},{16,0},{32,16},{48,32},{1,49},{17,1},{33,17},{49,33},{2,50}... | collective-permute-start | bytes 417800 | tf_op jit(solution)/shard_map/ppermute | solution.py:44
  199.0 3.6 %collective-permute-done.28.two = bf16[272,256]{1,0:T(8,128)(2,1)S(1)} collective-permute-done((bf16[272,256]{1,0:T(8,128)(2,1)S(1)}, bf16[272,256]{1,0:T(8,128)(2,1)S(1)}, u32[]{:S(2)}, u32[]{:S(2)}) %collective-permute-start.28) | collective-permute-done | bytes 139296 | tf_op jit(solution)/shard_map/ppermute | solution.py:44
  (116 shorter events, 66.5 us)
Async XLA Ops:
  1.6 22.0 %collective-permute-start = (bf16[8192,256]{1,0:T(8,128)(2,1)}, bf16[8192,256]{1,0:T(8,128)(2,1)}, u32[]{:S(2)}, u32[]{:S(2)}) collective-permute-start(bf16[8192,256]{1,0:T(8,128)(2,1)} %own.1), channel_id=1, source_target_pairs={{0,8},{8,0},{1,9},{9,1},{2,10},{10,2},{3,11},{11,3},{4,12},{12,4},... | collective-permute-start | bytes 12582920 | tf_op jit(solution)/shard_map/ppermute | solution.py:44
  1.7 13.1 %collective-permute-start.1 = (bf16[256,256]{1,0:T(8,128)(2,1)S(1)}, bf16[256,256]{1,0:T(8,128)(2,1)S(1)}, u32[]{:S(2)}, u32[]{:S(2)}) collective-permute-start(bf16[256,256]{1,0:T(8,128)(2,1)S(1)} %shard_map.156.refs_2_), channel_id=1, source_target_pairs={{0,16},{16,32},{32,48},{48,0},{1,17},{17,33},{33,49},{49,1},{2,18}... | collective-permute-start | bytes 393224 | tf_op jit(solution)/shard_map/ppermute | solution.py:44
  5.1 15.1 %collective-permute-start.3 = (bf16[256,256]{1,0:T(8,128)(2,1)S(1)}, bf16[256,256]{1,0:T(8,128)(2,1)S(1)}, u32[]{:S(2)}, u32[]{:S(2)}) collective-permute-start(bf16[256,256]{1,0:T(8,128)(2,1)S(1)} %shard_map.156.refs_2_), channel_id=1, source_target_pairs={{0,48},{16,0},{32,16},{48,32},{1,49},{17,1},{33,17},{49,33},{2,50}... | collective-permute-start | bytes 393224 | tf_op jit(solution)/shard_map/ppermute | solution.py:44
  7.3 16.3 %collective-permute-start.2 = (bf16[256,256]{1,0:T(8,128)(2,1)S(1)}, bf16[256,256]{1,0:T(8,128)(2,1)S(1)}, u32[]{:S(2)}, u32[]{:S(2)}) collective-permute-start(bf16[256,256]{1,0:T(8,128)(2,1)S(1)} %shard_map.156.refs_2_), channel_id=1, source_target_pairs={{0,32},{16,48},{32,0},{48,16},{1,33},{17,49},{33,1},{49,17},{2,34}... | collective-permute-start | bytes 393224 | tf_op jit(solution)/shard_map/ppermute | solution.py:44
  24.3 13.9 %collective-permute-start.6 = (bf16[256,1024]{1,0:T(8,128)(2,1)S(1)}, bf16[256,1024]{1,0:T(8,128)(2,1)S(1)}, u32[]{:S(2)}, u32[]{:S(2)}) collective-permute-start(bf16[256,1024]{1,0:T(8,128)(2,1)S(1)} %shard_map.158.p0), channel_id=1, source_target_pairs={{0,192},{64,0},{128,64},{192,128},{1,193},{65,1},{129,65},{193,129... | collective-permute-start | bytes 1572872 | tf_op jit(solution)/shard_map/ppermute | solution.py:44
  27.1 14.8 %collective-permute-start.4 = (bf16[256,1024]{1,0:T(8,128)(2,1)S(1)}, bf16[256,1024]{1,0:T(8,128)(2,1)S(1)}, u32[]{:S(2)}, u32[]{:S(2)}) collective-permute-start(bf16[256,1024]{1,0:T(8,128)(2,1)S(1)} %shard_map.158.p0), channel_id=1, source_target_pairs={{0,64},{64,128},{128,192},{192,0},{1,65},{65,129},{129,193},{193,1... | collective-permute-start | bytes 1572872 | tf_op jit(solution)/shard_map/ppermute | solution.py:44
  27.1 15.0 %all-to-all-start = ((bf16[8,64,256]{2,1,0:T(8,128)(2,1)}), bf16[8,64,256]{2,1,0:T(8,128)(2,1)S(1)}, u32[]{:S(2)}, u32[]{:S(2)}) async-start(bf16[8,64,256]{2,1,0:T(8,128)(2,1)} %bitcast.6.refs_0_), calls=%async_computation | async-start | bytes 524288 | tf_op jit(solution)/shard_map/all_to_all | solution.py:351
  38.1 21.3 %collective-permute-start.7 = (bf16[128,1024]{1,0:T(8,128)(2,1)S(1)}, bf16[128,1024]{1,0:T(8,128)(2,1)S(1)}, u32[]{:S(2)}, u32[]{:S(2)}) collective-permute-start(bf16[128,1024]{1,0:T(8,128)(2,1)S(1)} %slice.19), channel_id=1, source_target_pairs={{0,192},{64,0},{128,64},{192,128},{1,193},{65,1},{129,65},{193,129... | collective-permute-start | bytes 786440 | tf_op jit(solution)/shard_map/ppermute | solution.py:44
  41.9 17.5 %collective-permute-start.5 = (bf16[128,1024]{1,0:T(8,128)(2,1)S(1)}, bf16[128,1024]{1,0:T(8,128)(2,1)S(1)}, u32[]{:S(2)}, u32[]{:S(2)}) collective-permute-start(bf16[128,1024]{1,0:T(8,128)(2,1)S(1)} %slice.18), channel_id=1, source_target_pairs={{0,64},{64,128},{128,192},{192,0},{1,65},{65,129},{129,193},{193,1... | collective-permute-start | bytes 786440 | tf_op jit(solution)/shard_map/ppermute | solution.py:44
  42.9 14.1 %collective-permute-start.9 = (bf16[320,256]{1,0:T(8,128)(2,1)S(1)}, bf16[320,256]{1,0:T(8,128)(2,1)S(1)}, u32[]{:S(2)}, u32[]{:S(2)}) collective-permute-start(bf16[320,256]{1,0:T(8,128)(2,1)S(1)} %shard_map.160.refs_3_), channel_id=1, source_target_pairs={{0,32},{16,48},{32,0},{48,16},{1,33},{17,49},{33,1},{49,17},{2,34}... | collective-permute-start | bytes 491528 | tf_op jit(solution)/shard_map/ppermute | solution.py:44
  45.5 13.9 %collective-permute-start.8 = (bf16[320,256]{1,0:T(8,128)(2,1)S(1)}, bf16[320,256]{1,0:T(8,128)(2,1)S(1)}, u32[]{:S(2)}, u32[]{:S(2)}) collective-permute-start(bf16[320,256]{1,0:T(8,128)(2,1)S(1)} %shard_map.160.refs_3_), channel_id=1, source_target_pairs={{0,16},{16,32},{32,48},{48,0},{1,17},{17,33},{33,49},{49,1},{2,18}... | collective-permute-start | bytes 491528 | tf_op jit(solution)/shard_map/ppermute | solution.py:44
  60.1 17.2 %collective-permute-start.18 = (bf16[320,1024]{1,0:T(8,128)(2,1)S(1)}, bf16[320,1024]{1,0:T(8,128)(2,1)S(1)}, u32[]{:S(2)}, u32[]{:S(2)}) collective-permute-start(bf16[320,1024]{1,0:T(8,128)(2,1)S(1)} %shard_map.161.dep.p0), channel_id=1, source_target_pairs={{0,192},{64,0},{128,64},{192,128},{1,193},{65,1},{129,65},{193,129... | collective-permute-start | bytes 1966088 | tf_op jit(solution)/shard_map/ppermute | solution.py:44
  63.1 18.0 %collective-permute-start.16 = (bf16[320,1024]{1,0:T(8,128)(2,1)S(1)}, bf16[320,1024]{1,0:T(8,128)(2,1)S(1)}, u32[]{:S(2)}, u32[]{:S(2)}) collective-permute-start(bf16[320,1024]{1,0:T(8,128)(2,1)S(1)} %shard_map.161.dep.p0), channel_id=1, source_target_pairs={{0,64},{64,128},{128,192},{192,0},{1,65},{65,129},{129,193},{193,1... | collective-permute-start | bytes 1966088 | tf_op jit(solution)/shard_map/ppermute | solution.py:44
  67.8 13.4 %collective-permute-start.12 = (bf16[256,256]{1,0:T(8,128)(2,1)S(1)}, bf16[256,256]{1,0:T(8,128)(2,1)S(1)}, u32[]{:S(2)}, u32[]{:S(2)}) collective-permute-start(bf16[256,256]{1,0:T(8,128)(2,1)S(1)} %shard_map.163.here), channel_id=1, source_target_pairs={{0,4},{4,0},{1,5},{5,1},{2,6},{6,2},{3,7},{7,3},{8,12},{12,8},{9,1... | collective-permute-start | bytes 393224 | tf_op jit(solution)/shard_map/ppermute | solution.py:44
  77.3 23.2 %collective-permute-start.19 = (bf16[160,1024]{1,0:T(8,128)(2,1)S(1)}, bf16[160,1024]{1,0:T(8,128)(2,1)S(1)}, u32[]{:S(2)}, u32[]{:S(2)}) collective-permute-start(bf16[160,1024]{1,0:T(8,128)(2,1)S(1)} %slice.21), channel_id=1, source_target_pairs={{0,192},{64,0},{128,64},{192,128},{1,193},{65,1},{129,65},{193,129... | collective-permute-start | bytes 983048 | tf_op jit(solution)/shard_map/ppermute | solution.py:44
  81.1 19.4 %collective-permute-start.17 = (bf16[160,1024]{1,0:T(8,128)(2,1)S(1)}, bf16[160,1024]{1,0:T(8,128)(2,1)S(1)}, u32[]{:S(2)}, u32[]{:S(2)}) collective-permute-start(bf16[160,1024]{1,0:T(8,128)(2,1)S(1)} %slice.20), channel_id=1, source_target_pairs={{0,64},{64,128},{128,192},{192,0},{1,65},{65,129},{129,193},{193,1... | collective-permute-start | bytes 983048 | tf_op jit(solution)/shard_map/ppermute | solution.py:44
  81.8 13.3 %collective-permute-start.15 = (bf16[2,256,256]{2,1,0:T(8,128)(2,1)S(1)}, bf16[2,256,256]{2,1,0:T(8,128)(2,1)S(1)}, u32[]{:S(2)}, u32[]{:S(2)}) collective-permute-start(bf16[2,256,256]{2,1,0:T(8,128)(2,1)S(1)} %shard_map.164.s0), channel_id=1, source_target_pairs={{0,3},{1,0},{2,1},{3,2},{4,7},{5,4},{6,5},{7,6},{8,11},{9,8},{10,9... | collective-permute-start | bytes 786440 | tf_op jit(solution)/shard_map/ppermute | solution.py:44
  85.5 13.3 %collective-permute-start.13 = (bf16[2,256,256]{2,1,0:T(8,128)(2,1)S(1)}, bf16[2,256,256]{2,1,0:T(8,128)(2,1)S(1)}, u32[]{:S(2)}, u32[]{:S(2)}) collective-permute-start(bf16[2,256,256]{2,1,0:T(8,128)(2,1)S(1)} %shard_map.164.s0), channel_id=1, source_target_pairs={{0,1},{1,2},{2,3},{3,0},{4,5},{5,6},{6,7},{7,4},{8,9},{9,10},{10,1... | collective-permute-start | bytes 786440 | tf_op jit(solution)/shard_map/ppermute | solution.py:44
  133.1 18.0 %all-to-all-start.2 = ((bf16[8,256,256]{2,1,0:T(8,128)(2,1)}), bf16[8,256,256]{2,1,0:T(8,128)(2,1)S(1)}, u32[]{:S(2)}, u32[]{:S(2)}) async-start(bf16[8,256,256]{2,1,0:T(8,128)(2,1)} %copy-done.4), calls=%async_computation.2 | async-start | bytes 2097152 | tf_op jit(solution)/shard_map/all_to_all | solution.py:351
  138.0 13.9 %collective-permute-start.22 = (bf16[256,256]{1,0:T(8,128)(2,1)S(1)}, bf16[256,256]{1,0:T(8,128)(2,1)S(1)}, u32[]{:S(2)}, u32[]{:S(2)}) collective-permute-start(bf16[256,256]{1,0:T(8,128)(2,1)S(1)} %get-tuple-element.41.w_own), channel_id=1, source_target_pairs={{0,8},{8,0},{1,9},{9,1},{2,10},{10,2},{3,11},{11,3},{4,12},{12,4},... | collective-permute-start | bytes 393224 | tf_op jit(solution)/shard_map/ppermute | solution.py:44
  171.7 13.7 %collective-permute-start.25 = (bf16[1088,256]{1,0:T(8,128)(2,1)}, bf16[1088,256]{1,0:T(8,128)(2,1)S(1)}, u32[]{:S(2)}, u32[]{:S(2)}) collective-permute-start(bf16[1088,256]{1,0:T(8,128)(2,1)} %get-tuple-element.47), channel_id=1, source_target_pairs={{0,192},{64,0},{128,64},{192,128},{1,193},{65,1},{129,65},{193,129... | collective-permute-start | bytes 1671176 | tf_op jit(solution)/shard_map/ppermute | solution.py:44
  172.0 15.0 %collective-permute-start.26 = (bf16[1088,256]{1,0:T(8,128)(2,1)}, bf16[1088,256]{1,0:T(8,128)(2,1)S(1)}, u32[]{:S(2)}, u32[]{:S(2)}) collective-permute-start(bf16[1088,256]{1,0:T(8,128)(2,1)} %get-tuple-element.48), channel_id=1, source_target_pairs={{0,64},{64,128},{128,192},{192,0},{1,65},{65,129},{129,193},{193,1... | collective-permute-start | bytes 1671176 | tf_op jit(solution)/shard_map/ppermute | solution.py:44
  187.8 11.2 %collective-permute-start.27 = (bf16[272,256]{1,0:T(8,128)(2,1)S(1)}, bf16[272,256]{1,0:T(8,128)(2,1)S(1)}, u32[]{:S(2)}, u32[]{:S(2)}) collective-permute-start(bf16[272,256]{1,0:T(8,128)(2,1)S(1)} %get-tuple-element.50), channel_id=1, source_target_pairs={{0,48},{16,0},{32,16},{48,32},{1,49},{17,1},{33,17},{49,33},{2,50}... | collective-permute-start | bytes 417800 | tf_op jit(solution)/shard_map/ppermute | solution.py:44
  191.8 13.0 %collective-permute-start.29 = (bf16[272,256]{1,0:T(8,128)(2,1)S(1)}, bf16[272,256]{1,0:T(8,128)(2,1)S(1)}, u32[]{:S(2)}, u32[]{:S(2)}) collective-permute-start(bf16[272,256]{1,0:T(8,128)(2,1)S(1)} %get-tuple-element.52), channel_id=1, source_target_pairs={{0,16},{16,32},{32,48},{48,0},{1,17},{17,33},{33,49},{49,1},{2,18}... | collective-permute-start | bytes 417800 | tf_op jit(solution)/shard_map/ppermute | solution.py:44
  (24 other events, 384.8 us)

commit v2 on v1

--- a/solution.py
+++ b/solution.py
@@ -21,7 +21,7 @@
 X, Z, C, L, Y = range(5)
 f32 = jnp.float32
 bf16 = jnp.bfloat16
-VMEM_BYTES = 24 * 1024 * 1024
+VMEM_BYTES = 20 * 1024 * 1024
 
 
 def call(body, outs, position, *args, far=(), deps=(), scratch=(), space=pltpu.VMEM):
@@ -93,66 +93,55 @@
         out[:, i * piece.shape[1] : (i + 1) * piece.shape[1]] = piece[...]
 
 
-def basis_body(pos, own, other, out, sems):
-    size = out.shape[1] // 2
-
-    def copies(n):
-        place = pl.multiple_of((chip_place(pos, n // 4, n % 4) * 2 + pos[C]) * size, size)
-        slot = pl.ds(pl.multiple_of(n * size, size), size)
+def basis_body(pos, own, other, b0, b1, b2, b3, sems):
+    size = b0.shape[1] // 2
+
+    def copies(out, i, j):
+        place = pl.multiple_of((chip_place(pos, i, j) * 2 + pos[C]) * size, size)
+        slot = pl.ds(pl.multiple_of(j * size, size), size)
         return [
             pltpu.make_async_copy(
-                ref.at[pl.ds(place, size), :], out.at[slot, pl.ds(k * size, size)], sems.at[n, k]
+                ref.at[pl.ds(place, size), :], out.at[slot, pl.ds(k * size, size)], sems.at[i, j, k]
             )
             for k, ref in enumerate((own, other))
         ]
 
-    def start(n, carry):
-        for copy in copies(n):
-            copy.start()
-        return carry
-
-    def wait(n, carry):
-        for copy in copies(n):
-            copy.wait()
-        return carry
-
-    lax.fori_loop(0, 16, start, 0)
-    lax.fori_loop(0, 16, wait, 0)
-
-
-def basis_parts(basis, buf, sems, order):
-    deep = buf.shape[0] // 4
-    copies = {}
-    for i in order:
-        part = pl.ds(i * deep, deep)
-        copies[i] = pltpu.make_async_copy(basis.at[part, :], buf.at[part, :], sems.at[i])
-        copies[i].start()
-
-    def read(i):
-        copies[i].wait()
-        return buf[i * deep : (i + 1) * deep, :]
-
-    return read
-
-
-def left_body(pos, basis, dep, p0, p1, top, low, p3, keep, send, buf, sems):
+    outs = tuple(enumerate((b0, b1, b2, b3)))
+    for i, out in outs:
+
+        def start(j, carry, i=i, out=out):
+            for copy in copies(out, i, j):
+                copy.start()
+            return carry
+
+        lax.fori_loop(0, 4, start, 0)
+    for i, out in outs:
+
+        def wait(j, carry, i=i, out=out):
+            for copy in copies(out, i, j):
+                copy.wait()
+            return carry
+
+        lax.fori_loop(0, 4, wait, 0)
+
+
+def left_body(pos, dep, b0, b1, b2, b3, p0, p1, top, low, p3, keep, send):
     size = keep.shape[1]
-    read = basis_parts(basis, buf, sems, (0, 1, 3, 2))
     total = None
-    for i, piece in ((0, p0[...]), (1, p1[...]), (3, p3[...]), (2, None)):
+    for basis, piece in ((b0, p0[...]), (b1, p1[...]), (b3, p3[...]), (b2, None)):
         if piece is None:
             piece = jnp.concatenate([top[...], low[...]], 0)
-        part = dot(piece, read(i))
+        part = dot(piece, basis[...])
         total = part if total is None else total + part
-    keep[...] = total[:, :size]
-    send[...] = total[:, size:]
+    keep[...] = total[:, :size].astype(bf16)
+    send[...] = total[:, size:].astype(bf16)
 
 
 def left_tokens_body(
-    pos, basis, dep, gain, p0, p1, top, low, p3, keep, send, buf, sems, turned, first, square
+    pos, dep_a, dep_b, b0, b1, b2, b3, gain, p0, p1, top, low, p3, keep, send, turned, first, square
 ):
     cols = size = send.shape[1]
-    read = basis_parts(basis, buf, sems, (0, 1, 3, 2))
+    parts = (b0, b1, b2, b3)
     n_tok = p0.shape[0] - cols
     squares = 0.0
     total = None
@@ -166,7 +155,7 @@
         if i == 0:
             first[...] = feats[:, :size].reshape(first.shape)
         piece = jnp.concatenate([piece[:cols, :], feats.astype(bf16)], 0)
-        part = dot(piece, read(i))
+        part = dot(piece, parts[i][...])
         total = part if total is None else total + part
     keep[:cols, :] = total[:cols, :size]
     send[:cols, :] = total[:cols, size:]
@@ -182,13 +171,9 @@
             at += rows
 
 
-def left_sum_body(pos, keep, recv, out):
-    out[...] = (keep[...] + recv[...]).T.astype(bf16)
-
-
-def pair_body(pos, here, there, out):
-    out[0] = here[...]
-    out[1] = there[...]
+def pair_body(pos, keep, core, low, both, out):
+    out[0] = (keep[...].astype(f32) + core[...].astype(f32)).T.astype(bf16)
+    out[1] = (low[...].astype(f32) + both[...].astype(f32)).T.astype(bf16)
 
 
 def left_tokens_sum_body(pos, keep, recv, all_out, out):
@@ -242,8 +227,8 @@
     out[...] = sum(parts[n].astype(f32) for n in range(8)).astype(bf16)
 
 
-def update_far_body(pos, basis, back_own, back_other, kv, top, low, buf, sems, whole):
-    update_body((2,), pos, basis, back_own, back_other, kv, whole, buf, sems)
+def update_far_body(pos, back_own, back_other, kv, basis, top, low, whole):
+    update_body((2,), pos, back_own, back_other, kv, basis, whole)
     half = top.shape[0]
     top[...] = whole[:half, :]
     low[...] = whole[half:, :]
@@ -257,16 +242,15 @@
     o3[half:, :] = (three[half:, :].astype(f32) + low[...].astype(f32)).astype(bf16)
 
 
-def update_body(steps, pos, basis, back_own, back_other, kv, *refs):
+def update_body(steps, pos, back_own, back_other, kv, *refs):
     size = back_own.shape[0]
     rows = kv.shape[2]
     back = jnp.concatenate([back_own[...], back_other[...]], 0)
-    read = basis_parts(basis, refs[-2], refs[-1], steps)
-    for i, out in zip(steps, refs):
-        part = read(i)
+    many = len(steps)
+    for i, basis, out in zip(steps, refs[:many], refs[many:]):
         for n in range(0, 4, 2):
-            rows_here = slice(n * size, (n + 2) * size)
-            out[rows_here, :] = dot(part[rows_here, :], back).astype(bf16)
+            part = slice(n * size, (n + 2) * size)
+            out[part, :] = dot(basis[part, :], back).astype(bf16)
         for j in range(4):
             out[4 * size + j * rows : 4 * size + (j + 1) * rows, :] = kv[i, j]
 
@@ -352,13 +336,13 @@
 
 
 def ring_first(array):
+    return shift(array, "x", 1), shift(array, "x", -1)
+
+
+def ring_gather(array, first, dep):
+    one, three = first
     half = array.shape[0] // 2
-    one, three = shift(array, "x", 1), shift(array, "x", -1)
-    return one, three, one[:half], three[half:]
-
-
-def ring_gather(array, first):
-    one, three, top, low = first
+    top, low = after(one, dep[0])[:half], after(three, dep[-1])[half:]
     return [array, one, shift(top, "x", 1), shift(low, "x", -1), three]
 
 
@@ -406,15 +390,13 @@
     owner = lax.dynamic_index_in_dim(owner, group_at, 0, keepdims=False).reshape(-1, 1)
 
     q_other = swap(after(q_left, grad_t))
-    (basis,) = call(
+    basis = call(
         basis_body,
-        [((16 * rows, 2 * rows), bf16)],
+        [((4 * rows, 2 * rows), bf16)] * 4,
         position,
         far=(q_left, q_other),
-        scratch=[pltpu.SemaphoreType.DMA((16, 2))],
-        space=pltpu.HBM,
-    )
-    basis_scratch = [pltpu.VMEM(basis.shape, bf16), pltpu.SemaphoreType.DMA((4,))]
+        scratch=[pltpu.SemaphoreType.DMA((4, 4, 2))],
+    )
     moment_new, moment_t, master_low = call(
         moment_body,
         [(square, f32), ((cols, rows), bf16), (square, bf16)],
@@ -426,7 +408,6 @@
     deep = cols + n_tok // 8
     (grad_x,) = call(wide_body, [((cols, 4 * rows), bf16)], position, grad_t, *grad_z, deps=(picked, q_other))
     grad_first = ring_first(grad_x)
-    grad_pieces = ring_gather(grad_x, grad_first)
     (moment_z,) = call(
         moment_tokens_body,
         [((deep, rows), bf16)],
@@ -436,12 +417,12 @@
         owner,
     )
     moment_z = after(moment_z, grad_x)
+    grad_pieces = ring_gather(grad_x, grad_first, [moment_z])
     moment_others = others(moment_z, "zh")
     (moment_x,) = call(
-        wide_body, [((deep, 4 * rows), bf16)], position, moment_z, *moment_others, deps=(*grad_pieces[2:4], basis)
+        wide_body, [((deep, 4 * rows), bf16)], position, moment_z, *moment_others, deps=(*grad_pieces[2:4], basis[0])
     )
     moment_first = ring_first(moment_x)
-    moment_pieces = ring_gather(moment_x, moment_first)
 
     master_other = swap(master_low)
 
@@ -465,31 +446,36 @@
 
     keep, send = call(
         left_body,
-        [((cols, rows), f32)] * 2,
-        position,
+        [((cols, rows), bf16)] * 2,
+        position,
+        *basis,
         *grad_pieces,
-        far=(basis,),
         deps=(moment_x,),
-        scratch=basis_scratch,
-    )
-    (left_g,) = call(left_sum_body, [(square, bf16)], position, keep, swap(send))
+    )
     (left_g,) = call(
-        pair_body, [((2,) + square, bf16)], position, left_g, shift(left_g, "zl", 1)
-    )
+        pair_body,
+        [((2,) + square, bf16)],
+        position,
+        keep,
+        swap(send),
+        shift(keep, "zl", 1),
+        lax.ppermute(send, ("c", "zl"), [(i, 3 - i) for i in range(4)]),
+    )
+    left_others = others(left_g, "y")
     (variance_new,) = call(
-        variance_body, [(square, f32)], position, q_right, variance, left_g, *others(left_g, "y")
-    )
-
+        variance_body, [(square, f32)], position, q_right, variance, left_g, *left_others
+    )
+
+    moment_pieces = ring_gather(moment_x, moment_first, left_others[::2])
     keep, send = call(
         left_tokens_body,
         [((cols + n_tok // 4, rows), f32)] * 2,
         position,
+        *basis,
         gain.reshape(32, 1, rows),
         *moment_pieces,
-        far=(basis,),
-        deps=(variance_new,),
-        scratch=basis_scratch
-        + [
+        deps=(variance_new, master_other),
+        scratch=[
             pltpu.VMEM((2, 2, n_tok // 16, rows), f32),
             pltpu.VMEM((2, n_tok // 16, rows), f32),
             pltpu.VMEM((2, n_tok // 16, rows), f32),
@@ -530,8 +516,8 @@
         back_own,
         back_other,
         kv,
-        far=(basis,),
-        scratch=basis_scratch + [pltpu.VMEM((many, cols), bf16)],
+        basis[2],
+        scratch=[pltpu.VMEM((many, cols), bf16)],
     )
     top, low = shift(top, "x", -1), shift(low, "x", 1)
     one, three, zero = call(
@@ -541,8 +527,9 @@
         back_own,
         back_other,
         kv,
-        far=(basis,),
-        scratch=basis_scratch,
+        basis[1],
+        basis[3],
+        basis[0],
     )
     one, three = call(
         add_halves_body, [((many, cols), bf16)] * 2, position, one, three, top, low

time: 207 us -> 203 us (0.981)
  blocking collectives: 23.3 us -> 42.5 us
  waiting for transfers between devices: 82.7 us -> 72 us
  starting transfers between devices: 57.4 us -> 50.6 us
  local copies, waits for them, and re-layouts: 14.6 us -> 11.4 us
  Pallas kernels: 27.4 us -> 24.7 us
    all_to_all x1 -> x2, blocking collectives: 23.3 us -> 42.5 us  [exchange(): return lax.all_to_all(array, ('zl', 'y'), 0, 0, tiled=True)]
    all_to_all x2 -> x1, waiting for transfers between devices: 13.1 us -> 4.33 us  [exchange(): return lax.all_to_all(array, ('zl', 'y'), 0, 0, tiled=True)]
    all_to_all x2 -> x1, starting transfers between devices: 10.8 us -> 5.93 us  [exchange(): return lax.all_to_all(array, ('zl', 'y'), 0, 0, tiled=True)]
    unnamed x33 -> x27, local copies, waits for them, and re-layouts: 8.07 us -> 4.87 us
    pallas_call x20 -> x19, Pallas kernels: 27.3 us -> 24.6 us  [call(): pl.pallas_call(body, out_shape=[jax.ShapeDtypeStruct(shape, kind) for sha...]
  transfers between devices with their start and end apart: 32 -> 32, of which waited for: 20 -> 18; matrix products, arithmetic and copies ran while one was open for 4% -> 4% of each run, Pallas kernels for 7% -> 6%
where the time goes in v2:
time: 203 us
  waiting for transfers between devices  72 us (35%)
  starting transfers between devices  50.6 us (25%)
  blocking collectives  42.5 us (21%)
  Pallas kernels  24.7 us (12%)
  local copies, waits for them, and re-layouts  11.4 us (6%)
    ppermute x30, waiting for transfers between devices, shift(): lax.ppermute(array, axis, [(i, (i + by) % size) for i in range(size)])  67.7 us
    ppermute x30, starting transfers between devices, shift(): lax.ppermute(array, axis, [(i, (i + by) % size) for i in range(size)])  44.6 us
    all_to_all x2, blocking collectives, exchange(): return lax.all_to_all(array, ('zl', 'y'), 0, 0, tiled=True)  42.5 us
    pallas_call x19, Pallas kernels, call(): pl.pallas_call(body, out_shape=[jax.ShapeDtypeStruct(shape, kind) for sha...  24.6 us
    all_to_all x1, starting transfers between devices, exchange(): return lax.all_to_all(array, ('zl', 'y'), 0, 0, tiled=True)  5.93 us
    gather x1, local copies, waits for them, and re-layouts, shards(): embed.at[local_ids].get(mode='promise_in_bounds')  5.27 us
    unnamed x27, local copies, waits for them, and re-layouts  4.87 us
    all_to_all x1, waiting for transfers between devices, exchange(): return lax.all_to_all(array, ('zl', 'y'), 0, 0, tiled=True)  4.33 us
  transfers between devices with their start and end apart: 32, of which 18 were waited for; matrix products, arithmetic and copies ran while one was open for 4% of the time, Pallas kernels for 6%

profile of v2, /device:TPU:32, one launch (start us, length us, event | category | flops | bytes accessed | tf_op | source)
XLA Modules:
  0.0 202.5 jit_solution(11731587115374054740)
XLA Ops:
  1.7 3.3 %collective-permute-start = (bf16[256,256]{1,0:T(8,128)(2,1)S(1)}, bf16[256,256]{1,0:T(8,128)(2,1)S(1)}, u32[]{:S(2)}, u32[]{:S(2)}) collective-permute-start(bf16[256,256]{1,0:T(8,128)(2,1)S(1)} %shard_map.156.refs_2_), channel_id=1, source_target_pairs={{0,16},{16,32},{32,48},{48,0},{1,17},{17,33},{33,49},{49,1},{2,18}... | collective-permute-start | bytes 393224 | tf_op jit(solution)/shard_map/ppermute | solution.py:44
  7.3 4.9 %collective-permute-start.2 = (bf16[256,256]{1,0:T(8,128)(2,1)S(1)}, bf16[256,256]{1,0:T(8,128)(2,1)S(1)}, u32[]{:S(2)}, u32[]{:S(2)}) collective-permute-start(bf16[256,256]{1,0:T(8,128)(2,1)S(1)} %shard_map.156.refs_2_), channel_id=1, source_target_pairs={{0,32},{16,48},{32,0},{48,16},{1,33},{17,49},{33,1},{49,17},{2,34}... | collective-permute-start | bytes 393224 | tf_op jit(solution)/shard_map/ppermute | solution.py:44
  14.9 5.3 %gather_fusion = bf16[512,256]{1,0:T(8,128)(2,1)} fusion(bf16[9504,256]{1,0:T(8,128)(2,1)} %param.19, s32[1024]{0:T(1024)S(1)} %pad_clamp_fusion), kind=kCustom, calls=%fused_computation | custom fusion | bytes 526336 | tf_op jit(solution)/shard_map/gather | solution.py:387
  20.2 3.5 %collective-permute-done.2.refs_4_ = bf16[256,256]{1,0:T(8,128)(2,1)S(1)} collective-permute-done((bf16[256,256]{1,0:T(8,128)(2,1)S(1)}, bf16[256,256]{1,0:T(8,128)(2,1)S(1)}, u32[]{:S(2)}, u32[]{:S(2)}) %collective-permute-start.2) | collective-permute-done | bytes 131104 | tf_op jit(solution)/shard_map/ppermute | solution.py:44
  24.3 2.8 %collective-permute-start.6 = (bf16[256,1024]{1,0:T(8,128)(2,1)S(1)}, bf16[256,1024]{1,0:T(8,128)(2,1)S(1)}, u32[]{:S(2)}, u32[]{:S(2)}) collective-permute-start(bf16[256,1024]{1,0:T(8,128)(2,1)S(1)} %shard_map.157.p0), channel_id=1, source_target_pairs={{0,192},{64,0},{128,64},{192,128},{1,193},{65,1},{129,65},{193,129... | collective-permute-start | bytes 1572872 | tf_op jit(solution)/shard_map/ppermute | solution.py:44
  27.1 5.9 %all-to-all-start = ((bf16[8,64,256]{2,1,0:T(8,128)(2,1)}), bf16[8,64,256]{2,1,0:T(8,128)(2,1)S(1)}, u32[]{:S(2)}, u32[]{:S(2)}) async-start(bf16[8,64,256]{2,1,0:T(8,128)(2,1)} %bitcast.6.refs_0_), calls=%async_computation | async-start | bytes 524288 | tf_op jit(solution)/shard_map/all_to_all | solution.py:335
  34.5 4.3 %all-to-all-done.arrived = bf16[8,64,256]{2,1,0:T(8,128)(2,1)S(1)} async-done(((bf16[8,64,256]{2,1,0:T(8,128)(2,1)}), bf16[8,64,256]{2,1,0:T(8,128)(2,1)S(1)}, u32[]{:S(2)}, u32[]{:S(2)}) %all-to-all-start) | async-done | bytes 262176 | tf_op jit(solution)/shard_map/all_to_all | solution.py:335
  39.6 3.3 %collective-permute-start.7 = (bf16[128,1024]{1,0:T(8,128)(2,1)S(1)}, bf16[128,1024]{1,0:T(8,128)(2,1)S(1)}, u32[]{:S(2)}, u32[]{:S(2)}) collective-permute-start(bf16[128,1024]{1,0:T(8,128)(2,1)S(1)} %slice.13), channel_id=1, source_target_pairs={{0,192},{64,0},{128,64},{192,128},{1,193},{65,1},{129,65},{193,129... | collective-permute-start | bytes 786440 | tf_op jit(solution)/shard_map/ppermute | solution.py:44
  43.4 4.0 %collective-permute-start.9 = (bf16[320,256]{1,0:T(8,128)(2,1)S(1)}, bf16[320,256]{1,0:T(8,128)(2,1)S(1)}, u32[]{:S(2)}, u32[]{:S(2)}) collective-permute-start(bf16[320,256]{1,0:T(8,128)(2,1)S(1)} %shard_map.159.refs_3_), channel_id=1, source_target_pairs={{0,32},{16,48},{32,0},{48,16},{1,33},{17,49},{33,1},{49,17},{2,34}... | collective-permute-start | bytes 491528 | tf_op jit(solution)/shard_map/ppermute | solution.py:44
  56.5 5.5 %collective-permute-done.8.refs_4_.dep = bf16[320,256]{1,0:T(8,128)(2,1)S(1)} collective-permute-done((bf16[320,256]{1,0:T(8,128)(2,1)S(1)}, bf16[320,256]{1,0:T(8,128)(2,1)S(1)}, u32[]{:S(2)}, u32[]{:S(2)}) %collective-permute-start.8) | collective-permute-done | bytes 163872 | tf_op jit(solution)/shard_map/ppermute | solution.py:44
  62.7 2.8 %collective-permute-start.20 = (bf16[320,1024]{1,0:T(8,128)(2,1)S(1)}, bf16[320,1024]{1,0:T(8,128)(2,1)S(1)}, u32[]{:S(2)}, u32[]{:S(2)}) collective-permute-start(bf16[320,1024]{1,0:T(8,128)(2,1)S(1)} %shard_map.161.dep.p0), channel_id=1, source_target_pairs={{0,192},{64,0},{128,64},{192,128},{1,193},{65,1},{129,65},{193,129... | collective-permute-start | bytes 1966088 | tf_op jit(solution)/shard_map/ppermute | solution.py:44
  69.6 4.1 %collective-permute-done.12.low = bf16[256,256]{1,0:T(8,128)(2,1)S(1)} collective-permute-done((bf16[256,256]{1,0:T(8,128)(2,1)S(1)}, bf16[256,256]{1,0:T(8,128)(2,1)S(1)}, u32[]{:S(2)}, u32[]{:S(2)}) %collective-permute-start.12) | collective-permute-done | bytes 131104 | tf_op jit(solution)/shard_map/ppermute | solution.py:44
  76.5 6.7 %collective-permute-done.16.s3 = bf16[2,256,256]{2,1,0:T(8,128)(2,1)S(1)} collective-permute-done((bf16[2,256,256]{2,1,0:T(8,128)(2,1)S(1)}, bf16[2,256,256]{2,1,0:T(8,128)(2,1)S(1)}, u32[]{:S(2)}, u32[]{:S(2)}) %collective-permute-start.16) | collective-permute-done | bytes 262176 | tf_op jit(solution)/shard_map/ppermute | solution.py:44
  83.2 3.3 %collective-permute-start.21 = (bf16[160,1024]{1,0:T(8,128)(2,1)S(1)}, bf16[160,1024]{1,0:T(8,128)(2,1)S(1)}, u32[]{:S(2)}, u32[]{:S(2)}) collective-permute-start(bf16[160,1024]{1,0:T(8,128)(2,1)S(1)} %slice.15), channel_id=1, source_target_pairs={{0,192},{64,0},{128,64},{192,128},{1,193},{65,1},{129,65},{193,129... | collective-permute-start | bytes 983048 | tf_op jit(solution)/shard_map/ppermute | solution.py:44
  88.1 8.6 %collective-permute-done.15.s2 = bf16[2,256,256]{2,1,0:T(8,128)(2,1)S(1)} collective-permute-done((bf16[2,256,256]{2,1,0:T(8,128)(2,1)S(1)}, bf16[2,256,256]{2,1,0:T(8,128)(2,1)S(1)}, u32[]{:S(2)}, u32[]{:S(2)}) %collective-permute-start.15) | collective-permute-done | bytes 262176 | tf_op jit(solution)/shard_map/ppermute | solution.py:44
  104.0 24.7 %all_to_all.15.left = bf16[8,384,256]{2,1,0:T(8,128)(2,1)S(1)} all-to-all(bf16[8,384,256]{2,1,0:T(8,128)(2,1)S(1)} %shard_map.166), channel_id=1, replica_groups=mesh['x'=4,'zh'=4,'c'=2,'zl'=2,'y'=4] {'zl','y'}, dimensions={0} | all-to-all | bytes 3145728 | tf_op jit(solution)/shard_map/all_to_all | solution.py:335
  130.6 17.8 %all_to_all.16.parts = bf16[8,256,256]{2,1,0:T(8,128)(2,1)S(1)} all-to-all(bf16[8,256,256]{2,1,0:T(8,128)(2,1)S(1)} %shard_map.167), channel_id=1, replica_groups=mesh['x'=4,'zh'=4,'c'=2,'zl'=2,'y'=4] {'zl','y'}, dimensions={0} | all-to-all | bytes 2097152 | tf_op jit(solution)/shard_map/all_to_all | solution.py:335
  152.4 2.9 %collective-permute-start.24 = (bf16[544,256]{1,0:T(8,128)(2,1)S(1)}, bf16[544,256]{1,0:T(8,128)(2,1)S(1)}, u32[]{:S(2)}, u32[]{:S(2)}) collective-permute-start(bf16[544,256]{1,0:T(8,128)(2,1)S(1)} %get-tuple-element.61), channel_id=1, source_target_pairs={{0,192},{64,0},{128,64},{192,128},{1,193},{65,1},{129,65},{193,129... | collective-permute-start | bytes 835592 | tf_op jit(solution)/shard_map/ppermute | solution.py:44
  156.8 4.7 %collective-permute-done.24.top = bf16[544,256]{1,0:T(8,128)(2,1)S(1)} collective-permute-done((bf16[544,256]{1,0:T(8,128)(2,1)S(1)}, bf16[544,256]{1,0:T(8,128)(2,1)S(1)}, u32[]{:S(2)}, u32[]{:S(2)}) %collective-permute-start.24) | collective-permute-done | bytes 278560 | tf_op jit(solution)/shard_map/ppermute | solution.py:44
  161.5 3.4 %collective-permute-done.25.low = bf16[544,256]{1,0:T(8,128)(2,1)S(1)} collective-permute-done((bf16[544,256]{1,0:T(8,128)(2,1)S(1)}, bf16[544,256]{1,0:T(8,128)(2,1)S(1)}, u32[]{:S(2)}, u32[]{:S(2)}) %collective-permute-start.25) | collective-permute-done | bytes 278560 | tf_op jit(solution)/shard_map/ppermute | solution.py:44
  168.9 11.5 %collective-permute-done.26.b = bf16[1088,256]{1,0:T(8,128)(2,1)S(1)} collective-permute-done((bf16[1088,256]{1,0:T(8,128)(2,1)}, bf16[1088,256]{1,0:T(8,128)(2,1)S(1)}, u32[]{:S(2)}, u32[]{:S(2)}) %collective-permute-start.26) | collective-permute-done | bytes 557088 | tf_op jit(solution)/shard_map/ppermute | solution.py:44
  182.6 2.9 %collective-permute-start.28 = (bf16[272,256]{1,0:T(8,128)(2,1)S(1)}, bf16[272,256]{1,0:T(8,128)(2,1)S(1)}, u32[]{:S(2)}, u32[]{:S(2)}) collective-permute-start(bf16[272,256]{1,0:T(8,128)(2,1)S(1)} %get-tuple-element.66), channel_id=1, source_target_pairs={{0,48},{16,0},{32,16},{48,32},{1,49},{17,1},{33,17},{49,33},{2,50}... | collective-permute-start | bytes 417800 | tf_op jit(solution)/shard_map/ppermute | solution.py:44
  189.9 2.9 %collective-permute-done.28.one = bf16[272,256]{1,0:T(8,128)(2,1)S(1)} collective-permute-done((bf16[272,256]{1,0:T(8,128)(2,1)S(1)}, bf16[272,256]{1,0:T(8,128)(2,1)S(1)}, u32[]{:S(2)}, u32[]{:S(2)}) %collective-permute-start.28) | collective-permute-done | bytes 139296 | tf_op jit(solution)/shard_map/ppermute | solution.py:44
  192.8 5.3 %collective-permute-done.29.two = bf16[272,256]{1,0:T(8,128)(2,1)S(1)} collective-permute-done((bf16[272,256]{1,0:T(8,128)(2,1)S(1)}, bf16[272,256]{1,0:T(8,128)(2,1)S(1)}, u32[]{:S(2)}, u32[]{:S(2)}) %collective-permute-start.29) | collective-permute-done | bytes 139296 | tf_op jit(solution)/shard_map/ppermute | solution.py:44
  (110 shorter events, 56.9 us)
Async XLA Ops:
  1.6 22.0 %collective-permute-start.1 = (bf16[8192,256]{1,0:T(8,128)(2,1)}, bf16[8192,256]{1,0:T(8,128)(2,1)}, u32[]{:S(2)}, u32[]{:S(2)}) collective-permute-start(bf16[8192,256]{1,0:T(8,128)(2,1)} %own.1), channel_id=1, source_target_pairs={{0,8},{8,0},{1,9},{9,1},{2,10},{10,2},{3,11},{11,3},{4,12},{12,4},... | collective-permute-start | bytes 12582920 | tf_op jit(solution)/shard_map/ppermute | solution.py:44
  1.7 13.1 %collective-permute-start = (bf16[256,256]{1,0:T(8,128)(2,1)S(1)}, bf16[256,256]{1,0:T(8,128)(2,1)S(1)}, u32[]{:S(2)}, u32[]{:S(2)}) collective-permute-start(bf16[256,256]{1,0:T(8,128)(2,1)S(1)} %shard_map.156.refs_2_), channel_id=1, source_target_pairs={{0,16},{16,32},{32,48},{48,0},{1,17},{17,33},{33,49},{49,1},{2,18}... | collective-permute-start | bytes 393224 | tf_op jit(solution)/shard_map/ppermute | solution.py:44
  5.1 15.1 %collective-permute-start.3 = (bf16[256,256]{1,0:T(8,128)(2,1)S(1)}, bf16[256,256]{1,0:T(8,128)(2,1)S(1)}, u32[]{:S(2)}, u32[]{:S(2)}) collective-permute-start(bf16[256,256]{1,0:T(8,128)(2,1)S(1)} %shard_map.156.refs_2_), channel_id=1, source_target_pairs={{0,48},{16,0},{32,16},{48,32},{1,49},{17,1},{33,17},{49,33},{2,50}... | collective-permute-start | bytes 393224 | tf_op jit(solution)/shard_map/ppermute | solution.py:44
  7.3 16.3 %collective-permute-start.2 = (bf16[256,256]{1,0:T(8,128)(2,1)S(1)}, bf16[256,256]{1,0:T(8,128)(2,1)S(1)}, u32[]{:S(2)}, u32[]{:S(2)}) collective-permute-start(bf16[256,256]{1,0:T(8,128)(2,1)S(1)} %shard_map.156.refs_2_), channel_id=1, source_target_pairs={{0,32},{16,48},{32,0},{48,16},{1,33},{17,49},{33,1},{49,17},{2,34}... | collective-permute-start | bytes 393224 | tf_op jit(solution)/shard_map/ppermute | solution.py:44
  24.3 15.3 %collective-permute-start.6 = (bf16[256,1024]{1,0:T(8,128)(2,1)S(1)}, bf16[256,1024]{1,0:T(8,128)(2,1)S(1)}, u32[]{:S(2)}, u32[]{:S(2)}) collective-permute-start(bf16[256,1024]{1,0:T(8,128)(2,1)S(1)} %shard_map.157.p0), channel_id=1, source_target_pairs={{0,192},{64,0},{128,64},{192,128},{1,193},{65,1},{129,65},{193,129... | collective-permute-start | bytes 1572872 | tf_op jit(solution)/shard_map/ppermute | solution.py:44
  27.1 15.8 %collective-permute-start.4 = (bf16[256,1024]{1,0:T(8,128)(2,1)S(1)}, bf16[256,1024]{1,0:T(8,128)(2,1)S(1)}, u32[]{:S(2)}, u32[]{:S(2)}) collective-permute-start(bf16[256,1024]{1,0:T(8,128)(2,1)S(1)} %shard_map.157.p0), channel_id=1, source_target_pairs={{0,64},{64,128},{128,192},{192,0},{1,65},{65,129},{129,193},{193,1... | collective-permute-start | bytes 1572872 | tf_op jit(solution)/shard_map/ppermute | solution.py:44
  27.1 11.8 %all-to-all-start = ((bf16[8,64,256]{2,1,0:T(8,128)(2,1)}), bf16[8,64,256]{2,1,0:T(8,128)(2,1)S(1)}, u32[]{:S(2)}, u32[]{:S(2)}) async-start(bf16[8,64,256]{2,1,0:T(8,128)(2,1)} %bitcast.6.refs_0_), calls=%async_computation | async-start | bytes 524288 | tf_op jit(solution)/shard_map/all_to_all | solution.py:335
  39.6 22.5 %collective-permute-start.7 = (bf16[128,1024]{1,0:T(8,128)(2,1)S(1)}, bf16[128,1024]{1,0:T(8,128)(2,1)S(1)}, u32[]{:S(2)}, u32[]{:S(2)}) collective-permute-start(bf16[128,1024]{1,0:T(8,128)(2,1)S(1)} %slice.13), channel_id=1, source_target_pairs={{0,192},{64,0},{128,64},{192,128},{1,193},{65,1},{129,65},{193,129... | collective-permute-start | bytes 786440 | tf_op jit(solution)/shard_map/ppermute | solution.py:44
  42.9 19.2 %collective-permute-start.5 = (bf16[128,1024]{1,0:T(8,128)(2,1)S(1)}, bf16[128,1024]{1,0:T(8,128)(2,1)S(1)}, u32[]{:S(2)}, u32[]{:S(2)}) collective-permute-start(bf16[128,1024]{1,0:T(8,128)(2,1)S(1)} %slice.12), channel_id=1, source_target_pairs={{0,64},{64,128},{128,192},{192,0},{1,65},{65,129},{129,193},{193,1... | collective-permute-start | bytes 786440 | tf_op jit(solution)/shard_map/ppermute | solution.py:44
  43.0 11.9 %collective-permute-start.10 = (bf16[320,256]{1,0:T(8,128)(2,1)S(1)}, bf16[320,256]{1,0:T(8,128)(2,1)S(1)}, u32[]{:S(2)}, u32[]{:S(2)}) collective-permute-start(bf16[320,256]{1,0:T(8,128)(2,1)S(1)} %shard_map.159.refs_3_), channel_id=1, source_target_pairs={{0,48},{16,0},{32,16},{48,32},{1,49},{17,1},{33,17},{49,33},{2,50}... | collective-permute-start | bytes 491528 | tf_op jit(solution)/shard_map/ppermute | solution.py:44
  43.4 13.2 %collective-permute-start.9 = (bf16[320,256]{1,0:T(8,128)(2,1)S(1)}, bf16[320,256]{1,0:T(8,128)(2,1)S(1)}, u32[]{:S(2)}, u32[]{:S(2)}) collective-permute-start(bf16[320,256]{1,0:T(8,128)(2,1)S(1)} %shard_map.159.refs_3_), channel_id=1, source_target_pairs={{0,32},{16,48},{32,0},{48,16},{1,33},{17,49},{33,1},{49,17},{2,34}... | collective-permute-start | bytes 491528 | tf_op jit(solution)/shard_map/ppermute | solution.py:44
  47.3 14.8 %collective-permute-start.8 = (bf16[320,256]{1,0:T(8,128)(2,1)S(1)}, bf16[320,256]{1,0:T(8,128)(2,1)S(1)}, u32[]{:S(2)}, u32[]{:S(2)}) collective-permute-start(bf16[320,256]{1,0:T(8,128)(2,1)S(1)} %shard_map.159.refs_3_), channel_id=1, source_target_pairs={{0,16},{16,32},{32,48},{48,0},{1,17},{17,33},{33,49},{49,1},{2,18}... | collective-permute-start | bytes 491528 | tf_op jit(solution)/shard_map/ppermute | solution.py:44
  62.7 20.5 %collective-permute-start.20 = (bf16[320,1024]{1,0:T(8,128)(2,1)S(1)}, bf16[320,1024]{1,0:T(8,128)(2,1)S(1)}, u32[]{:S(2)}, u32[]{:S(2)}) collective-permute-start(bf16[320,1024]{1,0:T(8,128)(2,1)S(1)} %shard_map.161.dep.p0), channel_id=1, source_target_pairs={{0,192},{64,0},{128,64},{192,128},{1,193},{65,1},{129,65},{193,129... | collective-permute-start | bytes 1966088 | tf_op jit(solution)/shard_map/ppermute | solution.py:44
  65.6 21.0 %collective-permute-start.18 = (bf16[320,1024]{1,0:T(8,128)(2,1)S(1)}, bf16[320,1024]{1,0:T(8,128)(2,1)S(1)}, u32[]{:S(2)}, u32[]{:S(2)}) collective-permute-start(bf16[320,1024]{1,0:T(8,128)(2,1)S(1)} %shard_map.161.dep.p0), channel_id=1, source_target_pairs={{0,64},{64,128},{128,192},{192,0},{1,65},{65,129},{129,193},{193,1... | collective-permute-start | bytes 1966088 | tf_op jit(solution)/shard_map/ppermute | solution.py:44
  76.0 10.6 %collective-permute-start.14 = (bf16[2,256,256]{2,1,0:T(8,128)(2,1)S(1)}, bf16[2,256,256]{2,1,0:T(8,128)(2,1)S(1)}, u32[]{:S(2)}, u32[]{:S(2)}) collective-permute-start(bf16[2,256,256]{2,1,0:T(8,128)(2,1)S(1)} %shard_map.163.s0), channel_id=1, source_target_pairs={{0,1},{1,2},{2,3},{3,0},{4,5},{5,6},{6,7},{7,4},{8,9},{9,10},{10,1... | collective-permute-start | bytes 786440 | tf_op jit(solution)/shard_map/ppermute | solution.py:44
  83.2 15.3 %collective-permute-start.21 = (bf16[160,1024]{1,0:T(8,128)(2,1)S(1)}, bf16[160,1024]{1,0:T(8,128)(2,1)S(1)}, u32[]{:S(2)}, u32[]{:S(2)}) collective-permute-start(bf16[160,1024]{1,0:T(8,128)(2,1)S(1)} %slice.15), channel_id=1, source_target_pairs={{0,192},{64,0},{128,64},{192,128},{1,193},{65,1},{129,65},{193,129... | collective-permute-start | bytes 983048 | tf_op jit(solution)/shard_map/ppermute | solution.py:44
  86.5 11.9 %collective-permute-start.19 = (bf16[160,1024]{1,0:T(8,128)(2,1)S(1)}, bf16[160,1024]{1,0:T(8,128)(2,1)S(1)}, u32[]{:S(2)}, u32[]{:S(2)}) collective-permute-start(bf16[160,1024]{1,0:T(8,128)(2,1)S(1)} %slice.14), channel_id=1, source_target_pairs={{0,64},{64,128},{128,192},{192,0},{1,65},{65,129},{129,193},{193,1... | collective-permute-start | bytes 983048 | tf_op jit(solution)/shard_map/ppermute | solution.py:44
  86.6 10.1 %collective-permute-start.15 = (bf16[2,256,256]{2,1,0:T(8,128)(2,1)S(1)}, bf16[2,256,256]{2,1,0:T(8,128)(2,1)S(1)}, u32[]{:S(2)}, u32[]{:S(2)}) collective-permute-start(bf16[2,256,256]{2,1,0:T(8,128)(2,1)S(1)} %shard_map.163.s0), channel_id=1, source_target_pairs={{0,2},{1,3},{2,0},{3,1},{4,6},{5,7},{6,4},{7,5},{8,10},{9,11},{10,... | collective-permute-start | bytes 786440 | tf_op jit(solution)/shard_map/ppermute | solution.py:44
  88.1 10.4 %collective-permute-start.17 = (bf16[256,256]{1,0:T(8,128)(2,1)S(1)}, bf16[256,256]{1,0:T(8,128)(2,1)S(1)}, u32[]{:S(2)}, u32[]{:S(2)}) collective-permute-start(bf16[256,256]{1,0:T(8,128)(2,1)S(1)} %get-tuple-element.53.w_own), channel_id=1, source_target_pairs={{0,8},{8,0},{1,9},{9,1},{2,10},{10,2},{3,11},{11,3},{4,12},{12,4},... | collective-permute-start | bytes 393224 | tf_op jit(solution)/shard_map/ppermute | solution.py:44
  166.6 13.7 %collective-permute-start.26 = (bf16[1088,256]{1,0:T(8,128)(2,1)}, bf16[1088,256]{1,0:T(8,128)(2,1)S(1)}, u32[]{:S(2)}, u32[]{:S(2)}) collective-permute-start(bf16[1088,256]{1,0:T(8,128)(2,1)} %get-tuple-element.63), channel_id=1, source_target_pairs={{0,192},{64,0},{128,64},{192,128},{1,193},{65,1},{129,65},{193,129... | collective-permute-start | bytes 1671176 | tf_op jit(solution)/shard_map/ppermute | solution.py:44
  166.9 15.0 %collective-permute-start.27 = (bf16[1088,256]{1,0:T(8,128)(2,1)}, bf16[1088,256]{1,0:T(8,128)(2,1)S(1)}, u32[]{:S(2)}, u32[]{:S(2)}) collective-permute-start(bf16[1088,256]{1,0:T(8,128)(2,1)} %get-tuple-element.64), channel_id=1, source_target_pairs={{0,64},{64,128},{128,192},{192,0},{1,65},{65,129},{129,193},{193,1... | collective-permute-start | bytes 1671176 | tf_op jit(solution)/shard_map/ppermute | solution.py:44
  182.6 10.2 %collective-permute-start.28 = (bf16[272,256]{1,0:T(8,128)(2,1)S(1)}, bf16[272,256]{1,0:T(8,128)(2,1)S(1)}, u32[]{:S(2)}, u32[]{:S(2)}) collective-permute-start(bf16[272,256]{1,0:T(8,128)(2,1)S(1)} %get-tuple-element.66), channel_id=1, source_target_pairs={{0,48},{16,0},{32,16},{48,32},{1,49},{17,1},{33,17},{49,33},{2,50}... | collective-permute-start | bytes 417800 | tf_op jit(solution)/shard_map/ppermute | solution.py:44
  185.5 12.6 %collective-permute-start.29 = (bf16[272,256]{1,0:T(8,128)(2,1)S(1)}, bf16[272,256]{1,0:T(8,128)(2,1)S(1)}, u32[]{:S(2)}, u32[]{:S(2)}) collective-permute-start(bf16[272,256]{1,0:T(8,128)(2,1)S(1)} %get-tuple-element.67), channel_id=1, source_target_pairs={{0,32},{16,48},{32,0},{48,16},{1,33},{17,49},{33,1},{49,17},{2,34}... | collective-permute-start | bytes 417800 | tf_op jit(solution)/shard_map/ppermute | solution.py:44
  187.0 13.5 %collective-permute-start.30 = (bf16[272,256]{1,0:T(8,128)(2,1)S(1)}, bf16[272,256]{1,0:T(8,128)(2,1)S(1)}, u32[]{:S(2)}, u32[]{:S(2)}) collective-permute-start(bf16[272,256]{1,0:T(8,128)(2,1)S(1)} %get-tuple-element.68), channel_id=1, source_target_pairs={{0,16},{16,32},{32,48},{48,0},{1,17},{17,33},{33,49},{49,1},{2,18}... | collective-permute-start | bytes 417800 | tf_op jit(solution)/shard_map/ppermute | solution.py:44
  (21 other events, 315.6 us)

commit v3 on v2

--- a/solution.py
+++ b/solution.py
@@ -197,7 +197,7 @@
         all_out[n] = out[...]
 
 
-def variance_body(pos, right, variance, s0, s1, s2, s3, out):
+def new_variance(pos, right, variance, s0, s1, s2, s3):
     cols = right.shape[1]
     rot = None
     for j, piece in enumerate((s0, s1, s2, s3)):
@@ -206,11 +206,12 @@
             rows = pl.ds(pl.multiple_of(place * cols, cols), cols)
             part = dot(piece[i], right[rows, :])
             rot = part if rot is None else rot + part
-    out[...] = beta_two * variance[...] + (1.0 - beta_two) * rot * rot
-
-
-def direction_body(pos, right, variance_new, left, out):
+    return beta_two * variance[...] + (1.0 - beta_two) * rot * rot
+
+
+def direction_body(pos, right, variance, s0, s1, s2, s3, left, variance_new, out):
     cols = right.shape[1]
+    variance_new[...] = new_variance(pos, right, variance, s0, s1, s2, s3)
     rot = None
     for n in range(8):
         part = dot(left[n, :cols, :], right[n * cols : (n + 1) * cols, :])
@@ -462,10 +463,6 @@
         lax.ppermute(send, ("c", "zl"), [(i, 3 - i) for i in range(4)]),
     )
     left_others = others(left_g, "y")
-    (variance_new,) = call(
-        variance_body, [(square, f32)], position, q_right, variance, left_g, *left_others
-    )
-
     moment_pieces = ring_gather(moment_x, moment_first, left_others[::2])
     keep, send = call(
         left_tokens_body,
@@ -474,7 +471,7 @@
         *basis,
         gain.reshape(32, 1, rows),
         *moment_pieces,
-        deps=(variance_new, master_other),
+        deps=(left_others[1], master_other),
         scratch=[
             pltpu.VMEM((2, 2, n_tok // 16, rows), f32),
             pltpu.VMEM((2, n_tok // 16, rows), f32),
@@ -491,8 +488,15 @@
     )
     left_m = exchange(left_m)
 
-    (parts,) = call(
-        direction_body, [((8,) + square, bf16)], position, q_right, variance_new, left_m
+    variance_new, parts = call(
+        direction_body,
+        [(square, f32), ((8,) + square, bf16)],
+        position,
+        q_right,
+        variance,
+        left_g,
+        *left_others,
+        left_m,
     )
     (back_own,) = call(back_body, [(square, bf16)], position, exchange(parts))
     back_other = swap(back_own)

time: 203 us -> 200 us (0.985)
    pallas_call x19 -> x18, Pallas kernels: 24.6 us -> 23.1 us  [call(): pl.pallas_call(body, out_shape=[jax.ShapeDtypeStruct(shape, kind) for sha...]
    unnamed x27 -> x25, local copies, waits for them, and re-layouts: 4.87 us -> 3.93 us
  transfers between devices with their start and end apart: 32 -> 32, of which waited for: 18 -> 20; matrix products, arithmetic and copies ran while one was open for 4% -> 4% of each run, Pallas kernels for 6% -> 5%
where the time goes in v3:
time: 200 us
  waiting for transfers between devices  72.8 us (36%)
  starting transfers between devices  49.7 us (25%)
  blocking collectives  42.5 us (21%)
  Pallas kernels  23.2 us (12%)
  local copies, waits for them, and re-layouts  10.5 us (5%)
    ppermute x30, waiting for transfers between devices, shift(): lax.ppermute(array, axis, [(i, (i + by) % size) for i in range(size)])  68.5 us
    ppermute x30, starting transfers between devices, shift(): lax.ppermute(array, axis, [(i, (i + by) % size) for i in range(size)])  43.8 us
    all_to_all x2, blocking collectives, exchange(): return lax.all_to_all(array, ('zl', 'y'), 0, 0, tiled=True)  42.5 us
    pallas_call x18, Pallas kernels, call(): pl.pallas_call(body, out_shape=[jax.ShapeDtypeStruct(shape, kind) for sha...  23.1 us
    all_to_all x1, starting transfers between devices, exchange(): return lax.all_to_all(array, ('zl', 'y'), 0, 0, tiled=True)  5.93 us
    gather x1, local copies, waits for them, and re-layouts, shards(): embed.at[local_ids].get(mode='promise_in_bounds')  5.27 us
    all_to_all x1, waiting for transfers between devices, exchange(): return lax.all_to_all(array, ('zl', 'y'), 0, 0, tiled=True)  4.33 us
  transfers between devices with their start and end apart: 32, of which 20 were waited for; matrix products, arithmetic and copies ran while one was open for 4% of the time, Pallas kernels for 5%

profile of v3, /device:TPU:32, one launch (start us, length us, event | category | flops | bytes accessed | tf_op | source)
XLA Modules:
  0.0 200.1 jit_solution(15538037388382676382)
XLA Ops:
  1.7 3.3 %collective-permute-start = (bf16[256,256]{1,0:T(8,128)(2,1)S(1)}, bf16[256,256]{1,0:T(8,128)(2,1)S(1)}, u32[]{:S(2)}, u32[]{:S(2)}) collective-permute-start(bf16[256,256]{1,0:T(8,128)(2,1)S(1)} %shard_map.156.refs_2_), channel_id=1, source_target_pairs={{0,16},{16,32},{32,48},{48,0},{1,17},{17,33},{33,49},{49,1},{2,18}... | collective-permute-start | bytes 393224 | tf_op jit(solution)/shard_map/ppermute | solution.py:44
  7.3 4.9 %collective-permute-start.2 = (bf16[256,256]{1,0:T(8,128)(2,1)S(1)}, bf16[256,256]{1,0:T(8,128)(2,1)S(1)}, u32[]{:S(2)}, u32[]{:S(2)}) collective-permute-start(bf16[256,256]{1,0:T(8,128)(2,1)S(1)} %shard_map.156.refs_2_), channel_id=1, source_target_pairs={{0,32},{16,48},{32,0},{48,16},{1,33},{17,49},{33,1},{49,17},{2,34}... | collective-permute-start | bytes 393224 | tf_op jit(solution)/shard_map/ppermute | solution.py:44
  14.9 5.3 %gather_fusion = bf16[512,256]{1,0:T(8,128)(2,1)} fusion(bf16[9504,256]{1,0:T(8,128)(2,1)} %param.19, s32[1024]{0:T(1024)S(1)} %pad_clamp_fusion), kind=kCustom, calls=%fused_computation | custom fusion | bytes 526336 | tf_op jit(solution)/shard_map/gather | solution.py:388
  20.2 3.5 %collective-permute-done.2.refs_4_ = bf16[256,256]{1,0:T(8,128)(2,1)S(1)} collective-permute-done((bf16[256,256]{1,0:T(8,128)(2,1)S(1)}, bf16[256,256]{1,0:T(8,128)(2,1)S(1)}, u32[]{:S(2)}, u32[]{:S(2)}) %collective-permute-start.2) | collective-permute-done | bytes 131104 | tf_op jit(solution)/shard_map/ppermute | solution.py:44
  24.3 2.8 %collective-permute-start.6 = (bf16[256,1024]{1,0:T(8,128)(2,1)S(1)}, bf16[256,1024]{1,0:T(8,128)(2,1)S(1)}, u32[]{:S(2)}, u32[]{:S(2)}) collective-permute-start(bf16[256,1024]{1,0:T(8,128)(2,1)S(1)} %shard_map.157.p0), channel_id=1, source_target_pairs={{0,192},{64,0},{128,64},{192,128},{1,193},{65,1},{129,65},{193,129... | collective-permute-start | bytes 1572872 | tf_op jit(solution)/shard_map/ppermute | solution.py:44
  27.1 5.9 %all-to-all-start = ((bf16[8,64,256]{2,1,0:T(8,128)(2,1)}), bf16[8,64,256]{2,1,0:T(8,128)(2,1)S(1)}, u32[]{:S(2)}, u32[]{:S(2)}) async-start(bf16[8,64,256]{2,1,0:T(8,128)(2,1)} %bitcast.6.refs_0_), calls=%async_computation | async-start | bytes 524288 | tf_op jit(solution)/shard_map/all_to_all | solution.py:336
  34.5 4.3 %all-to-all-done.arrived = bf16[8,64,256]{2,1,0:T(8,128)(2,1)S(1)} async-done(((bf16[8,64,256]{2,1,0:T(8,128)(2,1)}), bf16[8,64,256]{2,1,0:T(8,128)(2,1)S(1)}, u32[]{:S(2)}, u32[]{:S(2)}) %all-to-all-start) | async-done | bytes 262176 | tf_op jit(solution)/shard_map/all_to_all | solution.py:336
  39.6 3.3 %collective-permute-start.7 = (bf16[128,1024]{1,0:T(8,128)(2,1)S(1)}, bf16[128,1024]{1,0:T(8,128)(2,1)S(1)}, u32[]{:S(2)}, u32[]{:S(2)}) collective-permute-start(bf16[128,1024]{1,0:T(8,128)(2,1)S(1)} %slice.13), channel_id=1, source_target_pairs={{0,192},{64,0},{128,64},{192,128},{1,193},{65,1},{129,65},{193,129... | collective-permute-start | bytes 786440 | tf_op jit(solution)/shard_map/ppermute | solution.py:44
  43.4 4.0 %collective-permute-start.9 = (bf16[320,256]{1,0:T(8,128)(2,1)S(1)}, bf16[320,256]{1,0:T(8,128)(2,1)S(1)}, u32[]{:S(2)}, u32[]{:S(2)}) collective-permute-start(bf16[320,256]{1,0:T(8,128)(2,1)S(1)} %shard_map.159.refs_3_), channel_id=1, source_target_pairs={{0,32},{16,48},{32,0},{48,16},{1,33},{17,49},{33,1},{49,17},{2,34}... | collective-permute-start | bytes 491528 | tf_op jit(solution)/shard_map/ppermute | solution.py:44
  50.4 2.5 %shard_map.160 = (bf16[1024,512]{1,0:T(8,128)(2,1)S(1)}, bf16[1024,512]{1,0:T(8,128)(2,1)S(1)}, bf16[1024,512]{1,0:T(8,128)(2,1)S(1)}, bf16[1024,512]{1,0:T(8,128)(2,1)S(1)}) custom-call(s32[9]{0:T(128)S(1)} %concatenate.9.pos, bf16[8192,256]{1,0:T(8,128)(2,1)S(1)} %copy-done, bf16[8192,256]{1,0:T(8,128)(2,1)} %collective-permute-done.1.refs_1_.other), custom_call_target="tpu_custom_call" | custom-call | tf_op jit(solution)/shard_map/pallas_call | solution.py:29
  56.5 5.5 %collective-permute-done.8.refs_4_.dep = bf16[320,256]{1,0:T(8,128)(2,1)S(1)} collective-permute-done((bf16[320,256]{1,0:T(8,128)(2,1)S(1)}, bf16[320,256]{1,0:T(8,128)(2,1)S(1)}, u32[]{:S(2)}, u32[]{:S(2)}) %collective-permute-start.8) | collective-permute-done | bytes 163872 | tf_op jit(solution)/shard_map/ppermute | solution.py:44
  62.7 2.8 %collective-permute-start.20 = (bf16[320,1024]{1,0:T(8,128)(2,1)S(1)}, bf16[320,1024]{1,0:T(8,128)(2,1)S(1)}, u32[]{:S(2)}, u32[]{:S(2)}) collective-permute-start(bf16[320,1024]{1,0:T(8,128)(2,1)S(1)} %shard_map.161.dep.p0), channel_id=1, source_target_pairs={{0,192},{64,0},{128,64},{192,128},{1,193},{65,1},{129,65},{193,129... | collective-permute-start | bytes 1966088 | tf_op jit(solution)/shard_map/ppermute | solution.py:44
  69.6 4.1 %collective-permute-done.12.low = bf16[256,256]{1,0:T(8,128)(2,1)S(1)} collective-permute-done((bf16[256,256]{1,0:T(8,128)(2,1)S(1)}, bf16[256,256]{1,0:T(8,128)(2,1)S(1)}, u32[]{:S(2)}, u32[]{:S(2)}) %collective-permute-start.12) | collective-permute-done | bytes 131104 | tf_op jit(solution)/shard_map/ppermute | solution.py:44
  76.5 6.7 %collective-permute-done.16.s3 = bf16[2,256,256]{2,1,0:T(8,128)(2,1)S(1)} collective-permute-done((bf16[2,256,256]{2,1,0:T(8,128)(2,1)S(1)}, bf16[2,256,256]{2,1,0:T(8,128)(2,1)S(1)}, u32[]{:S(2)}, u32[]{:S(2)}) %collective-permute-start.16) | collective-permute-done | bytes 262176 | tf_op jit(solution)/shard_map/ppermute | solution.py:44
  83.2 3.3 %collective-permute-start.21 = (bf16[160,1024]{1,0:T(8,128)(2,1)S(1)}, bf16[160,1024]{1,0:T(8,128)(2,1)S(1)}, u32[]{:S(2)}, u32[]{:S(2)}) collective-permute-start(bf16[160,1024]{1,0:T(8,128)(2,1)S(1)} %slice.15), channel_id=1, source_target_pairs={{0,192},{64,0},{128,64},{192,128},{1,193},{65,1},{129,65},{193,129... | collective-permute-start | bytes 983048 | tf_op jit(solution)/shard_map/ppermute | solution.py:44
  89.4 7.3 %collective-permute-done.15.dep_a.s2 = bf16[2,256,256]{2,1,0:T(8,128)(2,1)S(1)} collective-permute-done((bf16[2,256,256]{2,1,0:T(8,128)(2,1)S(1)}, bf16[2,256,256]{2,1,0:T(8,128)(2,1)S(1)}, u32[]{:S(2)}, u32[]{:S(2)}) %collective-permute-start.15) | collective-permute-done | bytes 262176 | tf_op jit(solution)/shard_map/ppermute | solution.py:44
  102.4 24.7 %all_to_all.15.left = bf16[8,384,256]{2,1,0:T(8,128)(2,1)S(1)} all-to-all(bf16[8,384,256]{2,1,0:T(8,128)(2,1)S(1)} %shard_map.165), channel_id=1, replica_groups=mesh['x'=4,'zh'=4,'c'=2,'zl'=2,'y'=4] {'zl','y'}, dimensions={0} | all-to-all | bytes 3145728 | tf_op jit(solution)/shard_map/all_to_all | solution.py:336
  129.1 17.8 %all_to_all.16.parts = bf16[8,256,256]{2,1,0:T(8,128)(2,1)S(1)} all-to-all(bf16[8,256,256]{2,1,0:T(8,128)(2,1)S(1)} %get-tuple-element.60), channel_id=1, replica_groups=mesh['x'=4,'zh'=4,'c'=2,'zl'=2,'y'=4] {'zl','y'}, dimensions={0} | all-to-all | bytes 2097152 | tf_op jit(solution)/shard_map/all_to_all | solution.py:336
  154.5 5.2 %collective-permute-done.24.top = bf16[544,256]{1,0:T(8,128)(2,1)S(1)} collective-permute-done((bf16[544,256]{1,0:T(8,128)(2,1)S(1)}, bf16[544,256]{1,0:T(8,128)(2,1)S(1)}, u32[]{:S(2)}, u32[]{:S(2)}) %collective-permute-start.24) | collective-permute-done | bytes 278560 | tf_op jit(solution)/shard_map/ppermute | solution.py:44
  159.7 2.8 %collective-permute-done.25.low = bf16[544,256]{1,0:T(8,128)(2,1)S(1)} collective-permute-done((bf16[544,256]{1,0:T(8,128)(2,1)S(1)}, bf16[544,256]{1,0:T(8,128)(2,1)S(1)}, u32[]{:S(2)}, u32[]{:S(2)}) %collective-permute-start.25) | collective-permute-done | bytes 278560 | tf_op jit(solution)/shard_map/ppermute | solution.py:44
  166.4 11.5 %collective-permute-done.26.b = bf16[1088,256]{1,0:T(8,128)(2,1)S(1)} collective-permute-done((bf16[1088,256]{1,0:T(8,128)(2,1)}, bf16[1088,256]{1,0:T(8,128)(2,1)S(1)}, u32[]{:S(2)}, u32[]{:S(2)}) %collective-permute-start.26) | collective-permute-done | bytes 557088 | tf_op jit(solution)/shard_map/ppermute | solution.py:44
  180.2 2.9 %collective-permute-start.28 = (bf16[272,256]{1,0:T(8,128)(2,1)S(1)}, bf16[272,256]{1,0:T(8,128)(2,1)S(1)}, u32[]{:S(2)}, u32[]{:S(2)}) collective-permute-start(bf16[272,256]{1,0:T(8,128)(2,1)S(1)} %get-tuple-element.69), channel_id=1, source_target_pairs={{0,48},{16,0},{32,16},{48,32},{1,49},{17,1},{33,17},{49,33},{2,50}... | collective-permute-start | bytes 417800 | tf_op jit(solution)/shard_map/ppermute | solution.py:44
  187.5 2.9 %collective-permute-done.28.one = bf16[272,256]{1,0:T(8,128)(2,1)S(1)} collective-permute-done((bf16[272,256]{1,0:T(8,128)(2,1)S(1)}, bf16[272,256]{1,0:T(8,128)(2,1)S(1)}, u32[]{:S(2)}, u32[]{:S(2)}) %collective-permute-start.28) | collective-permute-done | bytes 139296 | tf_op jit(solution)/shard_map/ppermute | solution.py:44
  190.4 5.3 %collective-permute-done.29.two = bf16[272,256]{1,0:T(8,128)(2,1)S(1)} collective-permute-done((bf16[272,256]{1,0:T(8,128)(2,1)S(1)}, bf16[272,256]{1,0:T(8,128)(2,1)S(1)}, u32[]{:S(2)}, u32[]{:S(2)}) %collective-permute-start.29) | collective-permute-done | bytes 139296 | tf_op jit(solution)/shard_map/ppermute | solution.py:44
  (107 shorter events, 56.3 us)
Async XLA Ops:
  1.6 22.0 %collective-permute-start.1 = (bf16[8192,256]{1,0:T(8,128)(2,1)}, bf16[8192,256]{1,0:T(8,128)(2,1)}, u32[]{:S(2)}, u32[]{:S(2)}) collective-permute-start(bf16[8192,256]{1,0:T(8,128)(2,1)} %own.1), channel_id=1, source_target_pairs={{0,8},{8,0},{1,9},{9,1},{2,10},{10,2},{3,11},{11,3},{4,12},{12,4},... | collective-permute-start | bytes 12582920 | tf_op jit(solution)/shard_map/ppermute | solution.py:44
  1.7 13.1 %collective-permute-start = (bf16[256,256]{1,0:T(8,128)(2,1)S(1)}, bf16[256,256]{1,0:T(8,128)(2,1)S(1)}, u32[]{:S(2)}, u32[]{:S(2)}) collective-permute-start(bf16[256,256]{1,0:T(8,128)(2,1)S(1)} %shard_map.156.refs_2_), channel_id=1, source_target_pairs={{0,16},{16,32},{32,48},{48,0},{1,17},{17,33},{33,49},{49,1},{2,18}... | collective-permute-start | bytes 393224 | tf_op jit(solution)/shard_map/ppermute | solution.py:44
  5.1 15.1 %collective-permute-start.3 = (bf16[256,256]{1,0:T(8,128)(2,1)S(1)}, bf16[256,256]{1,0:T(8,128)(2,1)S(1)}, u32[]{:S(2)}, u32[]{:S(2)}) collective-permute-start(bf16[256,256]{1,0:T(8,128)(2,1)S(1)} %shard_map.156.refs_2_), channel_id=1, source_target_pairs={{0,48},{16,0},{32,16},{48,32},{1,49},{17,1},{33,17},{49,33},{2,50}... | collective-permute-start | bytes 393224 | tf_op jit(solution)/shard_map/ppermute | solution.py:44
  7.3 16.3 %collective-permute-start.2 = (bf16[256,256]{1,0:T(8,128)(2,1)S(1)}, bf16[256,256]{1,0:T(8,128)(2,1)S(1)}, u32[]{:S(2)}, u32[]{:S(2)}) collective-permute-start(bf16[256,256]{1,0:T(8,128)(2,1)S(1)} %shard_map.156.refs_2_), channel_id=1, source_target_pairs={{0,32},{16,48},{32,0},{48,16},{1,33},{17,49},{33,1},{49,17},{2,34}... | collective-permute-start | bytes 393224 | tf_op jit(solution)/shard_map/ppermute | solution.py:44
  24.3 15.3 %collective-permute-start.6 = (bf16[256,1024]{1,0:T(8,128)(2,1)S(1)}, bf16[256,1024]{1,0:T(8,128)(2,1)S(1)}, u32[]{:S(2)}, u32[]{:S(2)}) collective-permute-start(bf16[256,1024]{1,0:T(8,128)(2,1)S(1)} %shard_map.157.p0), channel_id=1, source_target_pairs={{0,192},{64,0},{128,64},{192,128},{1,193},{65,1},{129,65},{193,129... | collective-permute-start | bytes 1572872 | tf_op jit(solution)/shard_map/ppermute | solution.py:44
  27.1 15.8 %collective-permute-start.4 = (bf16[256,1024]{1,0:T(8,128)(2,1)S(1)}, bf16[256,1024]{1,0:T(8,128)(2,1)S(1)}, u32[]{:S(2)}, u32[]{:S(2)}) collective-permute-start(bf16[256,1024]{1,0:T(8,128)(2,1)S(1)} %shard_map.157.p0), channel_id=1, source_target_pairs={{0,64},{64,128},{128,192},{192,0},{1,65},{65,129},{129,193},{193,1... | collective-permute-start | bytes 1572872 | tf_op jit(solution)/shard_map/ppermute | solution.py:44
  27.1 11.8 %all-to-all-start = ((bf16[8,64,256]{2,1,0:T(8,128)(2,1)}), bf16[8,64,256]{2,1,0:T(8,128)(2,1)S(1)}, u32[]{:S(2)}, u32[]{:S(2)}) async-start(bf16[8,64,256]{2,1,0:T(8,128)(2,1)} %bitcast.6.refs_0_), calls=%async_computation | async-start | bytes 524288 | tf_op jit(solution)/shard_map/all_to_all | solution.py:336
  39.6 22.5 %collective-permute-start.7 = (bf16[128,1024]{1,0:T(8,128)(2,1)S(1)}, bf16[128,1024]{1,0:T(8,128)(2,1)S(1)}, u32[]{:S(2)}, u32[]{:S(2)}) collective-permute-start(bf16[128,1024]{1,0:T(8,128)(2,1)S(1)} %slice.13), channel_id=1, source_target_pairs={{0,192},{64,0},{128,64},{192,128},{1,193},{65,1},{129,65},{193,129... | collective-permute-start | bytes 786440 | tf_op jit(solution)/shard_map/ppermute | solution.py:44
  42.9 19.2 %collective-permute-start.5 = (bf16[128,1024]{1,0:T(8,128)(2,1)S(1)}, bf16[128,1024]{1,0:T(8,128)(2,1)S(1)}, u32[]{:S(2)}, u32[]{:S(2)}) collective-permute-start(bf16[128,1024]{1,0:T(8,128)(2,1)S(1)} %slice.12), channel_id=1, source_target_pairs={{0,64},{64,128},{128,192},{192,0},{1,65},{65,129},{129,193},{193,1... | collective-permute-start | bytes 786440 | tf_op jit(solution)/shard_map/ppermute | solution.py:44
  43.0 11.9 %collective-permute-start.10 = (bf16[320,256]{1,0:T(8,128)(2,1)S(1)}, bf16[320,256]{1,0:T(8,128)(2,1)S(1)}, u32[]{:S(2)}, u32[]{:S(2)}) collective-permute-start(bf16[320,256]{1,0:T(8,128)(2,1)S(1)} %shard_map.159.refs_3_), channel_id=1, source_target_pairs={{0,48},{16,0},{32,16},{48,32},{1,49},{17,1},{33,17},{49,33},{2,50}... | collective-permute-start | bytes 491528 | tf_op jit(solution)/shard_map/ppermute | solution.py:44
  43.4 13.2 %collective-permute-start.9 = (bf16[320,256]{1,0:T(8,128)(2,1)S(1)}, bf16[320,256]{1,0:T(8,128)(2,1)S(1)}, u32[]{:S(2)}, u32[]{:S(2)}) collective-permute-start(bf16[320,256]{1,0:T(8,128)(2,1)S(1)} %shard_map.159.refs_3_), channel_id=1, source_target_pairs={{0,32},{16,48},{32,0},{48,16},{1,33},{17,49},{33,1},{49,17},{2,34}... | collective-permute-start | bytes 491528 | tf_op jit(solution)/shard_map/ppermute | solution.py:44
  47.3 14.8 %collective-permute-start.8 = (bf16[320,256]{1,0:T(8,128)(2,1)S(1)}, bf16[320,256]{1,0:T(8,128)(2,1)S(1)}, u32[]{:S(2)}, u32[]{:S(2)}) collective-permute-start(bf16[320,256]{1,0:T(8,128)(2,1)S(1)} %shard_map.159.refs_3_), channel_id=1, source_target_pairs={{0,16},{16,32},{32,48},{48,0},{1,17},{17,33},{33,49},{49,1},{2,18}... | collective-permute-start | bytes 491528 | tf_op jit(solution)/shard_map/ppermute | solution.py:44
  62.7 20.5 %collective-permute-start.20 = (bf16[320,1024]{1,0:T(8,128)(2,1)S(1)}, bf16[320,1024]{1,0:T(8,128)(2,1)S(1)}, u32[]{:S(2)}, u32[]{:S(2)}) collective-permute-start(bf16[320,1024]{1,0:T(8,128)(2,1)S(1)} %shard_map.161.dep.p0), channel_id=1, source_target_pairs={{0,192},{64,0},{128,64},{192,128},{1,193},{65,1},{129,65},{193,129... | collective-permute-start | bytes 1966088 | tf_op jit(solution)/shard_map/ppermute | solution.py:44
  65.6 21.0 %collective-permute-start.18 = (bf16[320,1024]{1,0:T(8,128)(2,1)S(1)}, bf16[320,1024]{1,0:T(8,128)(2,1)S(1)}, u32[]{:S(2)}, u32[]{:S(2)}) collective-permute-start(bf16[320,1024]{1,0:T(8,128)(2,1)S(1)} %shard_map.161.dep.p0), channel_id=1, source_target_pairs={{0,64},{64,128},{128,192},{192,0},{1,65},{65,129},{129,193},{193,1... | collective-permute-start | bytes 1966088 | tf_op jit(solution)/shard_map/ppermute | solution.py:44
  75.9 10.6 %collective-permute-start.14 = (bf16[2,256,256]{2,1,0:T(8,128)(2,1)S(1)}, bf16[2,256,256]{2,1,0:T(8,128)(2,1)S(1)}, u32[]{:S(2)}, u32[]{:S(2)}) collective-permute-start(bf16[2,256,256]{2,1,0:T(8,128)(2,1)S(1)} %shard_map.163.s0), channel_id=1, source_target_pairs={{0,1},{1,2},{2,3},{3,0},{4,5},{5,6},{6,7},{7,4},{8,9},{9,10},{10,1... | collective-permute-start | bytes 786440 | tf_op jit(solution)/shard_map/ppermute | solution.py:44
  83.2 13.6 %collective-permute-start.21 = (bf16[160,1024]{1,0:T(8,128)(2,1)S(1)}, bf16[160,1024]{1,0:T(8,128)(2,1)S(1)}, u32[]{:S(2)}, u32[]{:S(2)}) collective-permute-start(bf16[160,1024]{1,0:T(8,128)(2,1)S(1)} %slice.15), channel_id=1, source_target_pairs={{0,192},{64,0},{128,64},{192,128},{1,193},{65,1},{129,65},{193,129... | collective-permute-start | bytes 983048 | tf_op jit(solution)/shard_map/ppermute | solution.py:44
  86.5 11.2 %collective-permute-start.19 = (bf16[160,1024]{1,0:T(8,128)(2,1)S(1)}, bf16[160,1024]{1,0:T(8,128)(2,1)S(1)}, u32[]{:S(2)}, u32[]{:S(2)}) collective-permute-start(bf16[160,1024]{1,0:T(8,128)(2,1)S(1)} %slice.14), channel_id=1, source_target_pairs={{0,64},{64,128},{128,192},{192,0},{1,65},{65,129},{129,193},{193,1... | collective-permute-start | bytes 983048 | tf_op jit(solution)/shard_map/ppermute | solution.py:44
  86.6 10.1 %collective-permute-start.15 = (bf16[2,256,256]{2,1,0:T(8,128)(2,1)S(1)}, bf16[2,256,256]{2,1,0:T(8,128)(2,1)S(1)}, u32[]{:S(2)}, u32[]{:S(2)}) collective-permute-start(bf16[2,256,256]{2,1,0:T(8,128)(2,1)S(1)} %shard_map.163.s0), channel_id=1, source_target_pairs={{0,2},{1,3},{2,0},{3,1},{4,6},{5,7},{6,4},{7,5},{8,10},{9,11},{10,... | collective-permute-start | bytes 786440 | tf_op jit(solution)/shard_map/ppermute | solution.py:44
  152.8 9.6 %collective-permute-start.25 = (bf16[544,256]{1,0:T(8,128)(2,1)S(1)}, bf16[544,256]{1,0:T(8,128)(2,1)S(1)}, u32[]{:S(2)}, u32[]{:S(2)}) collective-permute-start(bf16[544,256]{1,0:T(8,128)(2,1)S(1)} %get-tuple-element.65), channel_id=1, source_target_pairs={{0,64},{64,128},{128,192},{192,0},{1,65},{65,129},{129,193},{193,1... | collective-permute-start | bytes 835592 | tf_op jit(solution)/shard_map/ppermute | solution.py:44
  164.2 13.7 %collective-permute-start.26 = (bf16[1088,256]{1,0:T(8,128)(2,1)}, bf16[1088,256]{1,0:T(8,128)(2,1)S(1)}, u32[]{:S(2)}, u32[]{:S(2)}) collective-permute-start(bf16[1088,256]{1,0:T(8,128)(2,1)} %get-tuple-element.66), channel_id=1, source_target_pairs={{0,192},{64,0},{128,64},{192,128},{1,193},{65,1},{129,65},{193,129... | collective-permute-start | bytes 1671176 | tf_op jit(solution)/shard_map/ppermute | solution.py:44
  164.4 15.0 %collective-permute-start.27 = (bf16[1088,256]{1,0:T(8,128)(2,1)}, bf16[1088,256]{1,0:T(8,128)(2,1)S(1)}, u32[]{:S(2)}, u32[]{:S(2)}) collective-permute-start(bf16[1088,256]{1,0:T(8,128)(2,1)} %get-tuple-element.67), channel_id=1, source_target_pairs={{0,64},{64,128},{128,192},{192,0},{1,65},{65,129},{129,193},{193,1... | collective-permute-start | bytes 1671176 | tf_op jit(solution)/shard_map/ppermute | solution.py:44
  180.2 10.2 %collective-permute-start.28 = (bf16[272,256]{1,0:T(8,128)(2,1)S(1)}, bf16[272,256]{1,0:T(8,128)(2,1)S(1)}, u32[]{:S(2)}, u32[]{:S(2)}) collective-permute-start(bf16[272,256]{1,0:T(8,128)(2,1)S(1)} %get-tuple-element.69), channel_id=1, source_target_pairs={{0,48},{16,0},{32,16},{48,32},{1,49},{17,1},{33,17},{49,33},{2,50}... | collective-permute-start | bytes 417800 | tf_op jit(solution)/shard_map/ppermute | solution.py:44
  183.1 12.7 %collective-permute-start.29 = (bf16[272,256]{1,0:T(8,128)(2,1)S(1)}, bf16[272,256]{1,0:T(8,128)(2,1)S(1)}, u32[]{:S(2)}, u32[]{:S(2)}) collective-permute-start(bf16[272,256]{1,0:T(8,128)(2,1)S(1)} %get-tuple-element.70), channel_id=1, source_target_pairs={{0,32},{16,48},{32,0},{48,16},{1,33},{17,49},{33,1},{49,17},{2,34}... | collective-permute-start | bytes 417800 | tf_op jit(solution)/shard_map/ppermute | solution.py:44
  184.5 13.5 %collective-permute-start.30 = (bf16[272,256]{1,0:T(8,128)(2,1)S(1)}, bf16[272,256]{1,0:T(8,128)(2,1)S(1)}, u32[]{:S(2)}, u32[]{:S(2)}) collective-permute-start(bf16[272,256]{1,0:T(8,128)(2,1)S(1)} %get-tuple-element.71), channel_id=1, source_target_pairs={{0,16},{16,32},{32,48},{48,0},{1,17},{17,33},{33,49},{49,1},{2,18}... | collective-permute-start | bytes 417800 | tf_op jit(solution)/shard_map/ppermute | solution.py:44
  (20 other events, 293.3 us)

commit v4 on v3

--- a/solution.py
+++ b/solution.py
@@ -228,8 +228,11 @@
     out[...] = sum(parts[n].astype(f32) for n in range(8)).astype(bf16)
 
 
-def update_far_body(pos, back_own, back_other, kv, basis, top, low, whole):
-    update_body((2,), pos, back_own, back_other, kv, basis, whole)
+def update_far_body(
+    pos, w_own, w_other, b_own, b_other, side, basis, top, low, kv, whole
+):
+    kv_body(pos, w_own, w_other, b_own, b_other, side, kv)
+    update_body((2,), pos, b_own, b_other, kv, basis, whole)
     half = top.shape[0]
     top[...] = whole[:half, :]
     low[...] = whole[half:, :]
@@ -237,10 +240,10 @@
 
 def add_halves_body(pos, one, three, top, low, o1, o3):
     half = top.shape[0]
-    o1[:half, :] = (one[:half, :].astype(f32) + top[...].astype(f32)).astype(bf16)
+    o1[:half, :] = one[:half, :] + top[...]
     o1[half:, :] = one[half:, :]
     o3[:half, :] = three[:half, :]
-    o3[half:, :] = (three[half:, :].astype(f32) + low[...].astype(f32)).astype(bf16)
+    o3[half:, :] = three[half:, :] + low[...]
 
 
 def update_body(steps, pos, back_own, back_other, kv, *refs):
@@ -501,25 +504,16 @@
     (back_own,) = call(back_body, [(square, bf16)], position, exchange(parts))
     back_other = swap(back_own)
 
-    (kv,) = call(
-        kv_body,
-        [((4, 4, tok_rows, cols), bf16)],
+    many = 4 * (rows + tok_rows)
+    top, low, kv = call(
+        update_far_body,
+        [((many // 2, cols), bf16)] * 2 + [((4, 4, tok_rows, cols), bf16)],
         position,
         master_low,
         master_other,
         back_own,
         back_other,
         left_m,
-    )
-
-    many = 4 * (rows + tok_rows)
-    top, low = call(
-        update_far_body,
-        [((many // 2, cols), bf16)] * 2,
-        position,
-        back_own,
-        back_other,
-        kv,
         basis[2],
         scratch=[pltpu.VMEM((many, cols), bf16)],
     )

time: 200 us -> 200 us (level)
    pallas_call x18 -> x17, Pallas kernels: 23.1 us -> 22.4 us  [call(): pl.pallas_call(body, out_shape=[jax.ShapeDtypeStruct(shape, kind) for sha...]
where the time goes in v4:
time: 200 us; the launch traced here: 199 us
  waiting for transfers between devices  72.8 us (36%)
  starting transfers between devices  49.7 us (25%)
  blocking collectives  42.5 us (21%)
  Pallas kernels  22.5 us (11%)
  local copies, waits for them, and re-layouts  10.5 us (5%)
    ppermute x30, waiting for transfers between devices, shift(): lax.ppermute(array, axis, [(i, (i + by) % size) for i in range(size)])  68.5 us
    ppermute x30, starting transfers between devices, shift(): lax.ppermute(array, axis, [(i, (i + by) % size) for i in range(size)])  43.8 us
    all_to_all x2, blocking collectives, exchange(): return lax.all_to_all(array, ('zl', 'y'), 0, 0, tiled=True)  42.5 us
    pallas_call x17, Pallas kernels, call(): pl.pallas_call(body, out_shape=[jax.ShapeDtypeStruct(shape, kind) for sha...  22.4 us
    all_to_all x1, starting transfers between devices, exchange(): return lax.all_to_all(array, ('zl', 'y'), 0, 0, tiled=True)  5.93 us
    gather x1, local copies, waits for them, and re-layouts, shards(): embed.at[local_ids].get(mode='promise_in_bounds')  5.27 us
    all_to_all x1, waiting for transfers between devices, exchange(): return lax.all_to_all(array, ('zl', 'y'), 0, 0, tiled=True)  4.33 us
  transfers between devices with their start and end apart: 32, of which 20 were waited for; matrix products, arithmetic and copies ran while one was open for 4% of the time, Pallas kernels for 5%

profile of v4, /device:TPU:32, one launch (start us, length us, event | category | flops | bytes accessed | tf_op | source)
XLA Modules:
  0.0 199.4 jit_solution(11654680833053386988)
XLA Ops:
  1.7 3.3 %collective-permute-start = (bf16[256,256]{1,0:T(8,128)(2,1)S(1)}, bf16[256,256]{1,0:T(8,128)(2,1)S(1)}, u32[]{:S(2)}, u32[]{:S(2)}) collective-permute-start(bf16[256,256]{1,0:T(8,128)(2,1)S(1)} %shard_map.156.refs_2_), channel_id=1, source_target_pairs={{0,16},{16,32},{32,48},{48,0},{1,17},{17,33},{33,49},{49,1},{2,18}... | collective-permute-start | bytes 393224 | tf_op jit(solution)/shard_map/ppermute | solution.py:44
  7.3 4.9 %collective-permute-start.2 = (bf16[256,256]{1,0:T(8,128)(2,1)S(1)}, bf16[256,256]{1,0:T(8,128)(2,1)S(1)}, u32[]{:S(2)}, u32[]{:S(2)}) collective-permute-start(bf16[256,256]{1,0:T(8,128)(2,1)S(1)} %shard_map.156.refs_2_), channel_id=1, source_target_pairs={{0,32},{16,48},{32,0},{48,16},{1,33},{17,49},{33,1},{49,17},{2,34}... | collective-permute-start | bytes 393224 | tf_op jit(solution)/shard_map/ppermute | solution.py:44
  14.9 5.3 %gather_fusion = bf16[512,256]{1,0:T(8,128)(2,1)} fusion(bf16[9504,256]{1,0:T(8,128)(2,1)} %param.19, s32[1024]{0:T(1024)S(1)} %pad_clamp_fusion), kind=kCustom, calls=%fused_computation | custom fusion | bytes 526336 | tf_op jit(solution)/shard_map/gather | solution.py:391
  20.2 3.5 %collective-permute-done.2.refs_4_ = bf16[256,256]{1,0:T(8,128)(2,1)S(1)} collective-permute-done((bf16[256,256]{1,0:T(8,128)(2,1)S(1)}, bf16[256,256]{1,0:T(8,128)(2,1)S(1)}, u32[]{:S(2)}, u32[]{:S(2)}) %collective-permute-start.2) | collective-permute-done | bytes 131104 | tf_op jit(solution)/shard_map/ppermute | solution.py:44
  24.3 2.8 %collective-permute-start.6 = (bf16[256,1024]{1,0:T(8,128)(2,1)S(1)}, bf16[256,1024]{1,0:T(8,128)(2,1)S(1)}, u32[]{:S(2)}, u32[]{:S(2)}) collective-permute-start(bf16[256,1024]{1,0:T(8,128)(2,1)S(1)} %shard_map.157.p0), channel_id=1, source_target_pairs={{0,192},{64,0},{128,64},{192,128},{1,193},{65,1},{129,65},{193,129... | collective-permute-start | bytes 1572872 | tf_op jit(solution)/shard_map/ppermute | solution.py:44
  27.1 5.9 %all-to-all-start = ((bf16[8,64,256]{2,1,0:T(8,128)(2,1)}), bf16[8,64,256]{2,1,0:T(8,128)(2,1)S(1)}, u32[]{:S(2)}, u32[]{:S(2)}) async-start(bf16[8,64,256]{2,1,0:T(8,128)(2,1)} %bitcast.6.refs_0_), calls=%async_computation | async-start | bytes 524288 | tf_op jit(solution)/shard_map/all_to_all | solution.py:339
  34.5 4.3 %all-to-all-done.arrived = bf16[8,64,256]{2,1,0:T(8,128)(2,1)S(1)} async-done(((bf16[8,64,256]{2,1,0:T(8,128)(2,1)}), bf16[8,64,256]{2,1,0:T(8,128)(2,1)S(1)}, u32[]{:S(2)}, u32[]{:S(2)}) %all-to-all-start) | async-done | bytes 262176 | tf_op jit(solution)/shard_map/all_to_all | solution.py:339
  39.6 3.3 %collective-permute-start.7 = (bf16[128,1024]{1,0:T(8,128)(2,1)S(1)}, bf16[128,1024]{1,0:T(8,128)(2,1)S(1)}, u32[]{:S(2)}, u32[]{:S(2)}) collective-permute-start(bf16[128,1024]{1,0:T(8,128)(2,1)S(1)} %slice.13), channel_id=1, source_target_pairs={{0,192},{64,0},{128,64},{192,128},{1,193},{65,1},{129,65},{193,129... | collective-permute-start | bytes 786440 | tf_op jit(solution)/shard_map/ppermute | solution.py:44
  43.4 4.0 %collective-permute-start.9 = (bf16[320,256]{1,0:T(8,128)(2,1)S(1)}, bf16[320,256]{1,0:T(8,128)(2,1)S(1)}, u32[]{:S(2)}, u32[]{:S(2)}) collective-permute-start(bf16[320,256]{1,0:T(8,128)(2,1)S(1)} %shard_map.159.refs_3_), channel_id=1, source_target_pairs={{0,32},{16,48},{32,0},{48,16},{1,33},{17,49},{33,1},{49,17},{2,34}... | collective-permute-start | bytes 491528 | tf_op jit(solution)/shard_map/ppermute | solution.py:44
  50.4 2.5 %shard_map.160 = (bf16[1024,512]{1,0:T(8,128)(2,1)S(1)}, bf16[1024,512]{1,0:T(8,128)(2,1)S(1)}, bf16[1024,512]{1,0:T(8,128)(2,1)S(1)}, bf16[1024,512]{1,0:T(8,128)(2,1)S(1)}) custom-call(s32[9]{0:T(128)S(1)} %concatenate.9.pos, bf16[8192,256]{1,0:T(8,128)(2,1)S(1)} %copy-done, bf16[8192,256]{1,0:T(8,128)(2,1)} %collective-permute-done.1.refs_1_.other), custom_call_target="tpu_custom_call" | custom-call | tf_op jit(solution)/shard_map/pallas_call | solution.py:29
  56.5 5.5 %collective-permute-done.8.refs_4_.dep = bf16[320,256]{1,0:T(8,128)(2,1)S(1)} collective-permute-done((bf16[320,256]{1,0:T(8,128)(2,1)S(1)}, bf16[320,256]{1,0:T(8,128)(2,1)S(1)}, u32[]{:S(2)}, u32[]{:S(2)}) %collective-permute-start.8) | collective-permute-done | bytes 163872 | tf_op jit(solution)/shard_map/ppermute | solution.py:44
  62.7 2.8 %collective-permute-start.20 = (bf16[320,1024]{1,0:T(8,128)(2,1)S(1)}, bf16[320,1024]{1,0:T(8,128)(2,1)S(1)}, u32[]{:S(2)}, u32[]{:S(2)}) collective-permute-start(bf16[320,1024]{1,0:T(8,128)(2,1)S(1)} %shard_map.161.dep.p0), channel_id=1, source_target_pairs={{0,192},{64,0},{128,64},{192,128},{1,193},{65,1},{129,65},{193,129... | collective-permute-start | bytes 1966088 | tf_op jit(solution)/shard_map/ppermute | solution.py:44
  69.6 4.1 %collective-permute-done.12.low = bf16[256,256]{1,0:T(8,128)(2,1)S(1)} collective-permute-done((bf16[256,256]{1,0:T(8,128)(2,1)S(1)}, bf16[256,256]{1,0:T(8,128)(2,1)S(1)}, u32[]{:S(2)}, u32[]{:S(2)}) %collective-permute-start.12) | collective-permute-done | bytes 131104 | tf_op jit(solution)/shard_map/ppermute | solution.py:44
  76.5 6.7 %collective-permute-done.16.s3 = bf16[2,256,256]{2,1,0:T(8,128)(2,1)S(1)} collective-permute-done((bf16[2,256,256]{2,1,0:T(8,128)(2,1)S(1)}, bf16[2,256,256]{2,1,0:T(8,128)(2,1)S(1)}, u32[]{:S(2)}, u32[]{:S(2)}) %collective-permute-start.16) | collective-permute-done | bytes 262176 | tf_op jit(solution)/shard_map/ppermute | solution.py:44
  83.2 3.3 %collective-permute-start.21 = (bf16[160,1024]{1,0:T(8,128)(2,1)S(1)}, bf16[160,1024]{1,0:T(8,128)(2,1)S(1)}, u32[]{:S(2)}, u32[]{:S(2)}) collective-permute-start(bf16[160,1024]{1,0:T(8,128)(2,1)S(1)} %slice.15), channel_id=1, source_target_pairs={{0,192},{64,0},{128,64},{192,128},{1,193},{65,1},{129,65},{193,129... | collective-permute-start | bytes 983048 | tf_op jit(solution)/shard_map/ppermute | solution.py:44
  89.4 7.3 %collective-permute-done.15.dep_a.s2 = bf16[2,256,256]{2,1,0:T(8,128)(2,1)S(1)} collective-permute-done((bf16[2,256,256]{2,1,0:T(8,128)(2,1)S(1)}, bf16[2,256,256]{2,1,0:T(8,128)(2,1)S(1)}, u32[]{:S(2)}, u32[]{:S(2)}) %collective-permute-start.15) | collective-permute-done | bytes 262176 | tf_op jit(solution)/shard_map/ppermute | solution.py:44
  102.4 24.7 %all_to_all.15.left.side = bf16[8,384,256]{2,1,0:T(8,128)(2,1)S(1)} all-to-all(bf16[8,384,256]{2,1,0:T(8,128)(2,1)S(1)} %shard_map.165), channel_id=1, replica_groups=mesh['x'=4,'zh'=4,'c'=2,'zl'=2,'y'=4] {'zl','y'}, dimensions={0} | all-to-all | bytes 3145728 | tf_op jit(solution)/shard_map/all_to_all | solution.py:339
  129.1 17.8 %all_to_all.16.parts = bf16[8,256,256]{2,1,0:T(8,128)(2,1)S(1)} all-to-all(bf16[8,256,256]{2,1,0:T(8,128)(2,1)S(1)} %get-tuple-element.61), channel_id=1, replica_groups=mesh['x'=4,'zh'=4,'c'=2,'zl'=2,'y'=4] {'zl','y'}, dimensions={0} | all-to-all | bytes 2097152 | tf_op jit(solution)/shard_map/all_to_all | solution.py:339
  153.8 5.2 %collective-permute-done.24.top = bf16[544,256]{1,0:T(8,128)(2,1)S(1)} collective-permute-done((bf16[544,256]{1,0:T(8,128)(2,1)S(1)}, bf16[544,256]{1,0:T(8,128)(2,1)S(1)}, u32[]{:S(2)}, u32[]{:S(2)}) %collective-permute-start.24) | collective-permute-done | bytes 278560 | tf_op jit(solution)/shard_map/ppermute | solution.py:44
  159.0 2.8 %collective-permute-done.25.low = bf16[544,256]{1,0:T(8,128)(2,1)S(1)} collective-permute-done((bf16[544,256]{1,0:T(8,128)(2,1)S(1)}, bf16[544,256]{1,0:T(8,128)(2,1)S(1)}, u32[]{:S(2)}, u32[]{:S(2)}) %collective-permute-start.25) | collective-permute-done | bytes 278560 | tf_op jit(solution)/shard_map/ppermute | solution.py:44
  165.7 11.5 %collective-permute-done.26.b = bf16[1088,256]{1,0:T(8,128)(2,1)S(1)} collective-permute-done((bf16[1088,256]{1,0:T(8,128)(2,1)}, bf16[1088,256]{1,0:T(8,128)(2,1)S(1)}, u32[]{:S(2)}, u32[]{:S(2)}) %collective-permute-start.26) | collective-permute-done | bytes 557088 | tf_op jit(solution)/shard_map/ppermute | solution.py:44
  179.5 2.9 %collective-permute-start.28 = (bf16[272,256]{1,0:T(8,128)(2,1)S(1)}, bf16[272,256]{1,0:T(8,128)(2,1)S(1)}, u32[]{:S(2)}, u32[]{:S(2)}) collective-permute-start(bf16[272,256]{1,0:T(8,128)(2,1)S(1)} %get-tuple-element.71), channel_id=1, source_target_pairs={{0,48},{16,0},{32,16},{48,32},{1,49},{17,1},{33,17},{49,33},{2,50}... | collective-permute-start | bytes 417800 | tf_op jit(solution)/shard_map/ppermute | solution.py:44
  186.8 2.9 %collective-permute-done.28.one = bf16[272,256]{1,0:T(8,128)(2,1)S(1)} collective-permute-done((bf16[272,256]{1,0:T(8,128)(2,1)S(1)}, bf16[272,256]{1,0:T(8,128)(2,1)S(1)}, u32[]{:S(2)}, u32[]{:S(2)}) %collective-permute-start.28) | collective-permute-done | bytes 139296 | tf_op jit(solution)/shard_map/ppermute | solution.py:44
  189.7 5.3 %collective-permute-done.29.two = bf16[272,256]{1,0:T(8,128)(2,1)S(1)} collective-permute-done((bf16[272,256]{1,0:T(8,128)(2,1)S(1)}, bf16[272,256]{1,0:T(8,128)(2,1)S(1)}, u32[]{:S(2)}, u32[]{:S(2)}) %collective-permute-start.29) | collective-permute-done | bytes 139296 | tf_op jit(solution)/shard_map/ppermute | solution.py:44
  (106 shorter events, 55.6 us)
Async XLA Ops:
  1.6 22.0 %collective-permute-start.1 = (bf16[8192,256]{1,0:T(8,128)(2,1)}, bf16[8192,256]{1,0:T(8,128)(2,1)}, u32[]{:S(2)}, u32[]{:S(2)}) collective-permute-start(bf16[8192,256]{1,0:T(8,128)(2,1)} %own.1), channel_id=1, source_target_pairs={{0,8},{8,0},{1,9},{9,1},{2,10},{10,2},{3,11},{11,3},{4,12},{12,4},... | collective-permute-start | bytes 12582920 | tf_op jit(solution)/shard_map/ppermute | solution.py:44
  1.7 13.1 %collective-permute-start = (bf16[256,256]{1,0:T(8,128)(2,1)S(1)}, bf16[256,256]{1,0:T(8,128)(2,1)S(1)}, u32[]{:S(2)}, u32[]{:S(2)}) collective-permute-start(bf16[256,256]{1,0:T(8,128)(2,1)S(1)} %shard_map.156.refs_2_), channel_id=1, source_target_pairs={{0,16},{16,32},{32,48},{48,0},{1,17},{17,33},{33,49},{49,1},{2,18}... | collective-permute-start | bytes 393224 | tf_op jit(solution)/shard_map/ppermute | solution.py:44
  5.1 15.1 %collective-permute-start.3 = (bf16[256,256]{1,0:T(8,128)(2,1)S(1)}, bf16[256,256]{1,0:T(8,128)(2,1)S(1)}, u32[]{:S(2)}, u32[]{:S(2)}) collective-permute-start(bf16[256,256]{1,0:T(8,128)(2,1)S(1)} %shard_map.156.refs_2_), channel_id=1, source_target_pairs={{0,48},{16,0},{32,16},{48,32},{1,49},{17,1},{33,17},{49,33},{2,50}... | collective-permute-start | bytes 393224 | tf_op jit(solution)/shard_map/ppermute | solution.py:44
  7.3 16.3 %collective-permute-start.2 = (bf16[256,256]{1,0:T(8,128)(2,1)S(1)}, bf16[256,256]{1,0:T(8,128)(2,1)S(1)}, u32[]{:S(2)}, u32[]{:S(2)}) collective-permute-start(bf16[256,256]{1,0:T(8,128)(2,1)S(1)} %shard_map.156.refs_2_), channel_id=1, source_target_pairs={{0,32},{16,48},{32,0},{48,16},{1,33},{17,49},{33,1},{49,17},{2,34}... | collective-permute-start | bytes 393224 | tf_op jit(solution)/shard_map/ppermute | solution.py:44
  24.3 15.3 %collective-permute-start.6 = (bf16[256,1024]{1,0:T(8,128)(2,1)S(1)}, bf16[256,1024]{1,0:T(8,128)(2,1)S(1)}, u32[]{:S(2)}, u32[]{:S(2)}) collective-permute-start(bf16[256,1024]{1,0:T(8,128)(2,1)S(1)} %shard_map.157.p0), channel_id=1, source_target_pairs={{0,192},{64,0},{128,64},{192,128},{1,193},{65,1},{129,65},{193,129... | collective-permute-start | bytes 1572872 | tf_op jit(solution)/shard_map/ppermute | solution.py:44
  27.1 15.8 %collective-permute-start.4 = (bf16[256,1024]{1,0:T(8,128)(2,1)S(1)}, bf16[256,1024]{1,0:T(8,128)(2,1)S(1)}, u32[]{:S(2)}, u32[]{:S(2)}) collective-permute-start(bf16[256,1024]{1,0:T(8,128)(2,1)S(1)} %shard_map.157.p0), channel_id=1, source_target_pairs={{0,64},{64,128},{128,192},{192,0},{1,65},{65,129},{129,193},{193,1... | collective-permute-start | bytes 1572872 | tf_op jit(solution)/shard_map/ppermute | solution.py:44
  27.1 11.8 %all-to-all-start = ((bf16[8,64,256]{2,1,0:T(8,128)(2,1)}), bf16[8,64,256]{2,1,0:T(8,128)(2,1)S(1)}, u32[]{:S(2)}, u32[]{:S(2)}) async-start(bf16[8,64,256]{2,1,0:T(8,128)(2,1)} %bitcast.6.refs_0_), calls=%async_computation | async-start | bytes 524288 | tf_op jit(solution)/shard_map/all_to_all | solution.py:339
  39.6 22.5 %collective-permute-start.7 = (bf16[128,1024]{1,0:T(8,128)(2,1)S(1)}, bf16[128,1024]{1,0:T(8,128)(2,1)S(1)}, u32[]{:S(2)}, u32[]{:S(2)}) collective-permute-start(bf16[128,1024]{1,0:T(8,128)(2,1)S(1)} %slice.13), channel_id=1, source_target_pairs={{0,192},{64,0},{128,64},{192,128},{1,193},{65,1},{129,65},{193,129... | collective-permute-start | bytes 786440 | tf_op jit(solution)/shard_map/ppermute | solution.py:44
  42.9 19.2 %collective-permute-start.5 = (bf16[128,1024]{1,0:T(8,128)(2,1)S(1)}, bf16[128,1024]{1,0:T(8,128)(2,1)S(1)}, u32[]{:S(2)}, u32[]{:S(2)}) collective-permute-start(bf16[128,1024]{1,0:T(8,128)(2,1)S(1)} %slice.12), channel_id=1, source_target_pairs={{0,64},{64,128},{128,192},{192,0},{1,65},{65,129},{129,193},{193,1... | collective-permute-start | bytes 786440 | tf_op jit(solution)/shard_map/ppermute | solution.py:44
  43.0 11.9 %collective-permute-start.10 = (bf16[320,256]{1,0:T(8,128)(2,1)S(1)}, bf16[320,256]{1,0:T(8,128)(2,1)S(1)}, u32[]{:S(2)}, u32[]{:S(2)}) collective-permute-start(bf16[320,256]{1,0:T(8,128)(2,1)S(1)} %shard_map.159.refs_3_), channel_id=1, source_target_pairs={{0,48},{16,0},{32,16},{48,32},{1,49},{17,1},{33,17},{49,33},{2,50}... | collective-permute-start | bytes 491528 | tf_op jit(solution)/shard_map/ppermute | solution.py:44
  43.4 13.2 %collective-permute-start.9 = (bf16[320,256]{1,0:T(8,128)(2,1)S(1)}, bf16[320,256]{1,0:T(8,128)(2,1)S(1)}, u32[]{:S(2)}, u32[]{:S(2)}) collective-permute-start(bf16[320,256]{1,0:T(8,128)(2,1)S(1)} %shard_map.159.refs_3_), channel_id=1, source_target_pairs={{0,32},{16,48},{32,0},{48,16},{1,33},{17,49},{33,1},{49,17},{2,34}... | collective-permute-start | bytes 491528 | tf_op jit(solution)/shard_map/ppermute | solution.py:44
  47.3 14.8 %collective-permute-start.8 = (bf16[320,256]{1,0:T(8,128)(2,1)S(1)}, bf16[320,256]{1,0:T(8,128)(2,1)S(1)}, u32[]{:S(2)}, u32[]{:S(2)}) collective-permute-start(bf16[320,256]{1,0:T(8,128)(2,1)S(1)} %shard_map.159.refs_3_), channel_id=1, source_target_pairs={{0,16},{16,32},{32,48},{48,0},{1,17},{17,33},{33,49},{49,1},{2,18}... | collective-permute-start | bytes 491528 | tf_op jit(solution)/shard_map/ppermute | solution.py:44
  62.7 20.5 %collective-permute-start.20 = (bf16[320,1024]{1,0:T(8,128)(2,1)S(1)}, bf16[320,1024]{1,0:T(8,128)(2,1)S(1)}, u32[]{:S(2)}, u32[]{:S(2)}) collective-permute-start(bf16[320,1024]{1,0:T(8,128)(2,1)S(1)} %shard_map.161.dep.p0), channel_id=1, source_target_pairs={{0,192},{64,0},{128,64},{192,128},{1,193},{65,1},{129,65},{193,129... | collective-permute-start | bytes 1966088 | tf_op jit(solution)/shard_map/ppermute | solution.py:44
  65.6 21.0 %collective-permute-start.18 = (bf16[320,1024]{1,0:T(8,128)(2,1)S(1)}, bf16[320,1024]{1,0:T(8,128)(2,1)S(1)}, u32[]{:S(2)}, u32[]{:S(2)}) collective-permute-start(bf16[320,1024]{1,0:T(8,128)(2,1)S(1)} %shard_map.161.dep.p0), channel_id=1, source_target_pairs={{0,64},{64,128},{128,192},{192,0},{1,65},{65,129},{129,193},{193,1... | collective-permute-start | bytes 1966088 | tf_op jit(solution)/shard_map/ppermute | solution.py:44
  75.9 10.6 %collective-permute-start.14 = (bf16[2,256,256]{2,1,0:T(8,128)(2,1)S(1)}, bf16[2,256,256]{2,1,0:T(8,128)(2,1)S(1)}, u32[]{:S(2)}, u32[]{:S(2)}) collective-permute-start(bf16[2,256,256]{2,1,0:T(8,128)(2,1)S(1)} %shard_map.163.s0), channel_id=1, source_target_pairs={{0,1},{1,2},{2,3},{3,0},{4,5},{5,6},{6,7},{7,4},{8,9},{9,10},{10,1... | collective-permute-start | bytes 786440 | tf_op jit(solution)/shard_map/ppermute | solution.py:44
  83.2 13.6 %collective-permute-start.21 = (bf16[160,1024]{1,0:T(8,128)(2,1)S(1)}, bf16[160,1024]{1,0:T(8,128)(2,1)S(1)}, u32[]{:S(2)}, u32[]{:S(2)}) collective-permute-start(bf16[160,1024]{1,0:T(8,128)(2,1)S(1)} %slice.15), channel_id=1, source_target_pairs={{0,192},{64,0},{128,64},{192,128},{1,193},{65,1},{129,65},{193,129... | collective-permute-start | bytes 983048 | tf_op jit(solution)/shard_map/ppermute | solution.py:44
  86.5 11.2 %collective-permute-start.19 = (bf16[160,1024]{1,0:T(8,128)(2,1)S(1)}, bf16[160,1024]{1,0:T(8,128)(2,1)S(1)}, u32[]{:S(2)}, u32[]{:S(2)}) collective-permute-start(bf16[160,1024]{1,0:T(8,128)(2,1)S(1)} %slice.14), channel_id=1, source_target_pairs={{0,64},{64,128},{128,192},{192,0},{1,65},{65,129},{129,193},{193,1... | collective-permute-start | bytes 983048 | tf_op jit(solution)/shard_map/ppermute | solution.py:44
  86.6 10.1 %collective-permute-start.15 = (bf16[2,256,256]{2,1,0:T(8,128)(2,1)S(1)}, bf16[2,256,256]{2,1,0:T(8,128)(2,1)S(1)}, u32[]{:S(2)}, u32[]{:S(2)}) collective-permute-start(bf16[2,256,256]{2,1,0:T(8,128)(2,1)S(1)} %shard_map.163.s0), channel_id=1, source_target_pairs={{0,2},{1,3},{2,0},{3,1},{4,6},{5,7},{6,4},{7,5},{8,10},{9,11},{10,... | collective-permute-start | bytes 786440 | tf_op jit(solution)/shard_map/ppermute | solution.py:44
  152.1 9.6 %collective-permute-start.25 = (bf16[544,256]{1,0:T(8,128)(2,1)S(1)}, bf16[544,256]{1,0:T(8,128)(2,1)S(1)}, u32[]{:S(2)}, u32[]{:S(2)}) collective-permute-start(bf16[544,256]{1,0:T(8,128)(2,1)S(1)} %get-tuple-element.67), channel_id=1, source_target_pairs={{0,64},{64,128},{128,192},{192,0},{1,65},{65,129},{129,193},{193,1... | collective-permute-start | bytes 835592 | tf_op jit(solution)/shard_map/ppermute | solution.py:44
  163.5 13.7 %collective-permute-start.26 = (bf16[1088,256]{1,0:T(8,128)(2,1)}, bf16[1088,256]{1,0:T(8,128)(2,1)S(1)}, u32[]{:S(2)}, u32[]{:S(2)}) collective-permute-start(bf16[1088,256]{1,0:T(8,128)(2,1)} %get-tuple-element.68), channel_id=1, source_target_pairs={{0,192},{64,0},{128,64},{192,128},{1,193},{65,1},{129,65},{193,129... | collective-permute-start | bytes 1671176 | tf_op jit(solution)/shard_map/ppermute | solution.py:44
  163.7 15.0 %collective-permute-start.27 = (bf16[1088,256]{1,0:T(8,128)(2,1)}, bf16[1088,256]{1,0:T(8,128)(2,1)S(1)}, u32[]{:S(2)}, u32[]{:S(2)}) collective-permute-start(bf16[1088,256]{1,0:T(8,128)(2,1)} %get-tuple-element.69), channel_id=1, source_target_pairs={{0,64},{64,128},{128,192},{192,0},{1,65},{65,129},{129,193},{193,1... | collective-permute-start | bytes 1671176 | tf_op jit(solution)/shard_map/ppermute | solution.py:44
  179.5 10.2 %collective-permute-start.28 = (bf16[272,256]{1,0:T(8,128)(2,1)S(1)}, bf16[272,256]{1,0:T(8,128)(2,1)S(1)}, u32[]{:S(2)}, u32[]{:S(2)}) collective-permute-start(bf16[272,256]{1,0:T(8,128)(2,1)S(1)} %get-tuple-element.71), channel_id=1, source_target_pairs={{0,48},{16,0},{32,16},{48,32},{1,49},{17,1},{33,17},{49,33},{2,50}... | collective-permute-start | bytes 417800 | tf_op jit(solution)/shard_map/ppermute | solution.py:44
  182.4 12.6 %collective-permute-start.29 = (bf16[272,256]{1,0:T(8,128)(2,1)S(1)}, bf16[272,256]{1,0:T(8,128)(2,1)S(1)}, u32[]{:S(2)}, u32[]{:S(2)}) collective-permute-start(bf16[272,256]{1,0:T(8,128)(2,1)S(1)} %get-tuple-element.72), channel_id=1, source_target_pairs={{0,32},{16,48},{32,0},{48,16},{1,33},{17,49},{33,1},{49,17},{2,34}... | collective-permute-start | bytes 417800 | tf_op jit(solution)/shard_map/ppermute | solution.py:44
  183.8 13.5 %collective-permute-start.30 = (bf16[272,256]{1,0:T(8,128)(2,1)S(1)}, bf16[272,256]{1,0:T(8,128)(2,1)S(1)}, u32[]{:S(2)}, u32[]{:S(2)}) collective-permute-start(bf16[272,256]{1,0:T(8,128)(2,1)S(1)} %get-tuple-element.73), channel_id=1, source_target_pairs={{0,16},{16,32},{32,48},{48,0},{1,17},{17,33},{33,49},{49,1},{2,18}... | collective-permute-start | bytes 417800 | tf_op jit(solution)/shard_map/ppermute | solution.py:44
  (20 other events, 290.0 us)
